TPU v7x, 512 devices: a whole 4x4x16 slice. The times are simulated.
512 devices in a mesh: sub: 64 (over z, x), crs: 8 (over y, core).
Axes of the slice: x: 4, y: 4, z: 16, core: 2. Of those that a mesh axis runs over, the one named last changes fastest.
Arguments:
- right_side: float32 [4, 64, 8, 384], P(None, 'sub', 'crs'), may hold values from -40 to 40
- own_block: bfloat16 [64, 8, 384, 384], P('sub', 'crs'), may hold values from -1 to 3
- coupling: bfloat16 [64, 8, 384, 768], P('sub', 'crs'), may hold values from -0.1875 to 0.1875
- local_inverse: bfloat16 [64, 8, 384, 1152], P('sub', 'crs'), may hold values from -1 to 3
- coarse_basis: float32 [64, 8, 40, 384], P('sub', 'crs'), may hold values from -0.3125 to 0.3125
- coarse_inverse: bfloat16 [64, 320, 8, 2560], P('sub', None, 'crs'), may hold values from -1 to 4
- neighbours: int32 [64, 8, 6], P('sub', 'crs'), may hold values from 0 to 63, as said below
- margin_rows: int32 [64, 8, 6, 128], P('sub', 'crs'), may hold values from 0 to 383, as said below
- block_counts: int32 [64, 8], P('sub', 'crs'), may hold values from 4 to 6, as said below
Outputs:
- solution: float32 [4, 64, 8, 384], P(None, 'sub', 'crs')
- basis_next: float32 [4, 64, 8, 384], P(None, 'sub', 'crs')
Inputs may be any that keep to these rules, and one draw needn't show every extreme that they name: A subdomain's listed neighbours are distinct sub indices other than its own; slot j of (s, c) names subdomain (neighbours[s, c, j], c). `margin_rows`: the rows of one block are distinct. `block_counts`: some subdomain uses all 6 slots.
All inputs are finite; a program needn't handle non-finite values.
Results may differ from a plain program's by a relative error of at most 0.0095.
Values may be sent and summed in bfloat16 or wider, within the bound.
No kernel may reach another device: no remote copies, remote signals or barrier semaphores. Data moves between devices by JAX's collectives and lax.ppermute only.
A program may use at most 64 MiB of HBM per device.

v0:
```python
import jax
import jax.numpy as jnp
from jax import lax
from jax.sharding import PartitionSpec as P

ITERS = 2


epsilon = 1e-06


def least_squares(start_norm, columns):
    cosines = []
    sine_terms = []
    triangle = []
    target = [start_norm] + [jnp.zeros_like(start_norm) for j in range(len(columns))]
    for j, column in enumerate(columns):
        column = list(column)
        for i in range(j):
            upper_value = cosines[i] * column[i] + sine_terms[i] * column[i + 1]
            column[i + 1] = -sine_terms[i] * column[i] + cosines[i] * column[i + 1]
            column[i] = upper_value
        radius = jnp.sqrt(column[j] * column[j] + column[j + 1] * column[j + 1])
        cosine = column[j] / radius
        sine_part = column[j + 1] / radius
        column[j] = radius
        target[j + 1] = -sine_part * target[j]
        target[j] = cosine * target[j]
        cosines.append(cosine)
        sine_terms.append(sine_part)
        triangle.append(column[: j + 1])
    weights = [None] * len(columns)
    for j in reversed(range(len(columns))):
        running = target[j]
        for k in range(j + 1, len(columns)):
            running = running - triangle[k][j] * weights[k]
        weights[j] = running / triangle[j][j]
    return weights


def body(
    right_side,
    own_block,
    coupling,
    local_inverse,
    coarse_basis,
    coarse_inverse,
    neighbours,
    margin_rows,
    block_counts,
):
    columns_count = right_side.shape[0]
    own_rows = right_side.shape[3]
    right_cols = right_side.reshape(columns_count, own_rows)
    own_matrix = own_block[0, 0]
    couple_matrix = coupling[0, 0]
    inverse = local_inverse[0, 0]
    basis_rows = coarse_basis[0, 0]
    coarse_rows = coarse_inverse[0, :, 0, :]
    listed = neighbours[0, 0]
    picked = margin_rows[0, 0]
    live_blocks = block_counts[0, 0]
    slot_count, block_rows = picked.shape
    sub_count = lax.axis_size("sub")
    all_rows = own_rows * sub_count * lax.axis_size("crs")
    live_slots = jnp.arange(slot_count) < live_blocks
    live_entries = jnp.repeat(live_slots, block_rows)
    contract_last = (((1,), (1,)), ((), ()))

    def neighbour_rows(vector_low):
        gathered = lax.all_gather(
            vector_low.reshape(columns_count, 1, own_rows), "sub", axis=1, tiled=True
        )
        flattened = gathered.reshape(columns_count, sub_count * own_rows)
        fetched = jnp.take(flattened, (listed[:, None] * own_rows + picked).reshape(-1), axis=1)
        return jnp.where(live_entries[None, :], fetched, jnp.zeros_like(fetched))

    start_norm = jnp.sqrt(
        lax.psum(jnp.sum(right_cols * right_cols, axis=1), ("sub", "crs")) / all_rows + epsilon
    )
    krylov = [right_cols / start_norm[:, None]]
    directions = []
    columns = []
    for j in range(ITERS):
        vector = krylov[j]
        precondition_vector_low = vector.astype(jnp.bfloat16)
        margin = neighbour_rows(precondition_vector_low)
        extended = jnp.concatenate([precondition_vector_low, margin], axis=1)
        fine_part = lax.dot_general(
            extended, inverse, contract_last, preferred_element_type=jnp.float32
        )
        restricted = lax.dot_general(
            basis_rows,
            vector,
            contract_last,
            precision=lax.Precision.HIGHEST,
            preferred_element_type=jnp.float32,
        )
        restricted_low = restricted.astype(jnp.bfloat16)
        partial_value = jnp.dot(
            coarse_rows,
            lax.all_gather(restricted_low, "sub", axis=0, tiled=True),
            preferred_element_type=jnp.float32,
        )
        solved = lax.psum_scatter(partial_value, "crs", scatter_dimension=0, tiled=True)
        coarse_part = lax.dot_general(
            solved,
            basis_rows,
            (((0,), (0,)), ((), ())),
            precision=lax.Precision.HIGHEST,
            preferred_element_type=jnp.float32,
        )
        direction = fine_part + coarse_part
        operate_vector_low = direction.astype(jnp.bfloat16)
        operate_margin = neighbour_rows(operate_vector_low)
        own_part = lax.dot_general(
            operate_vector_low, own_matrix, contract_last, preferred_element_type=jnp.float32
        )
        mapped = own_part + lax.dot_general(
            operate_margin, couple_matrix, contract_last, preferred_element_type=jnp.float32
        )
        local_terms = jnp.stack([jnp.sum(mapped * krylov[i], axis=1) for i in range(j + 1)])
        totals = lax.psum(local_terms, ("sub", "crs")) / all_rows
        heights = [totals[i] for i in range(j + 1)]
        for i in range(j + 1):
            mapped = mapped - heights[i][:, None] * krylov[i]
        length = jnp.sqrt(
            lax.psum(jnp.sum(mapped * mapped, axis=1), ("sub", "crs")) / all_rows + epsilon
        )
        columns.append(heights + [length])
        krylov.append(mapped / length[:, None])
        directions.append(direction)
    weights = least_squares(start_norm, columns)
    solution = weights[0][:, None] * directions[0]
    j = 1
    solution = solution + weights[j][:, None] * directions[j]
    return (
        solution.reshape(columns_count, 1, 1, own_rows),
        krylov[-1].reshape(columns_count, 1, 1, own_rows),
    )


def solution(mesh):
    in_specs = (
        P(None, "sub", "crs", None),
        P("sub", "crs", None, None),
        P("sub", "crs", None, None),
        P("sub", "crs", None, None),
        P("sub", "crs", None, None),
        P("sub", None, "crs", None),
        P("sub", "crs", None),
        P("sub", "crs", None, None),
        P("sub", "crs"),
    )
    out_specs = (P(None, "sub", "crs", None), P(None, "sub", "crs", None))
    return jax.shard_map(body, mesh=mesh, in_specs=in_specs, out_specs=out_specs, check_vma=False)
```

profile of v0, /device:TPU:1, one launch (start us, length us, event | category | flops | bytes accessed | tf_op | source)
XLA Modules:
  0.0 1068.9 jit_solution(1724894399045044511)
XLA Ops:
  0.6 0.0 copy-start
  0.6 0.0 copy-start.4
  0.7 0.0 copy-start.1
  0.7 0.0 copy-start.3
  0.7 0.8 reduce
  1.5 0.7 multiply_bitcast_fusion.1
  2.2 0.1 compare_and_fusion
  2.3 0.8 fusion.44
  3.1 111.0 %psum.35 = f32[4]{0:T(128)S(1)} all-reduce(f32[4]{0:T(128)S(1)} %fusion.44), channel_id=1, replica_groups=mesh['sub'=64,'crs'=8] {'sub','crs'}, use_global_device_ids=true, to_apply=%region_1.0 | all-reduce | flops 4 | bytes 32 | tf_op jit(solution)/shard_map/psum | solution.py:79
  114.1 0.8 fusion.45
  114.9 60.4 %all_gather.18 = bf16[4,64,384]{2,0,1:T(4,128)(2,1)S(1)} all-gather(bf16[4,1,384]{2,0,1:T(4,128)(2,1)S(1)} %fusion.45), channel_id=1, replica_groups=mesh['sub'=64,'crs'=8] {'sub'}, dimensions={1}, use_global_device_ids=true | all-gather | bytes 199680 | tf_op jit(solution)/shard_map/all_gather | solution.py:71
  175.3 4.7 copy.29
  180.0 5.2 gather_fusion
  185.9 0.1 broadcast_bitcast_fusion
  186.0 0.3 bitcast_select_fusion.5
  186.3 0.1 copy.30
  186.4 0.0 copy-done.4
  186.4 0.1 fusion.59
  186.5 0.0 copy-done.1
  186.5 0.4 fusion.14
  186.8 0.1 broadcast_divide_fusion
  186.9 0.0 copy-done.3
  186.9 0.2 fusion.10
  187.1 61.2 %all-gather.3 = bf16[64,40,4]{1,2,0:T(4,128)(2,1)S(1)} all-gather(bf16[1,40,4]{1,2,0:T(4,128)(2,1)S(1)} %fusion.10), channel_id=1, replica_groups=mesh['sub'=64,'crs'=8] {'sub'}, dimensions={0}, use_global_device_ids=true | all-gather | bytes 20800 | tf_op jit(solution)/shard_map/all_gather | solution.py:102
  248.3 0.1 reshape.154
  248.4 0.0 copy-done
  248.4 0.5 fusion.4
  249.0 51.3 %all-reduce = f32[320,4]{0,1:T(4,128)S(1)} all-reduce(f32[320,4]{0,1:T(4,128)S(1)} %fusion.4), channel_id=5, replica_groups=mesh['sub'=64,'crs'=8] {'crs'}, use_global_device_ids=true, to_apply=%region_2.0.clone | all-reduce | flops 1280 | bytes 10240
  300.3 1.3 dynamic-slice
  302.2 0.2 fusion.60
  302.4 60.3 %all-gather = bf16[4,24576]{1,0:T(4,128)(2,1)S(1)} all-gather(bf16[4,384]{1,0:T(4,128)(2,1)S(1)} %get-tuple-element.24), channel_id=2, replica_groups=mesh['sub'=64,'crs'=8] {'sub'}, dimensions={1}, use_global_device_ids=true | all-gather | bytes 199680 | tf_op jit(solution)/shard_map/all_gather | solution.py:71
  362.8 4.8 copy.32
  367.5 5.2 gather_fusion.1
  372.7 0.0 copy-done.2
  372.8 0.2 fusion.20
  372.9 1.7 multiply_reduce_fusion.4
  374.7 118.6 %psum.36 = f32[1,4]{1,0:T(1,128)S(1)} all-reduce(f32[1,4]{1,0:T(1,128)S(1)} %bitcast.148), channel_id=1, replica_groups=mesh['sub'=64,'crs'=8] {'sub','crs'}, use_global_device_ids=true, to_apply=%region_4.6 | all-reduce | flops 4 | bytes 32 | tf_op jit(solution)/shard_map/psum | solution.py:123
  493.3 0.2 multiply_reduce_fusion.3
  493.5 99.4 %psum.37 = f32[4]{0:T(128)S(1)} all-reduce(f32[4]{0:T(128)S(1)} %multiply_reduce_fusion.3), channel_id=1, replica_groups=mesh['sub'=64,'crs'=8] {'sub','crs'}, use_global_device_ids=true, to_apply=%region_6.8 | all-reduce | flops 4 | bytes 32 | tf_op jit(solution)/shard_map/psum | solution.py:128
  592.9 0.1 fusion.58
  593.0 61.1 %all-gather.1 = bf16[4,24576]{1,0:T(4,128)(2,1)S(1)} all-gather(bf16[4,384]{1,0:T(4,128)(2,1)S(1)} %get-tuple-element.15), channel_id=3, replica_groups=mesh['sub'=64,'crs'=8] {'sub'}, dimensions={1}, use_global_device_ids=true | all-gather | bytes 199680 | tf_op jit(solution)/shard_map/all_gather | solution.py:71
  654.1 4.8 copy.33
  658.9 5.2 gather_fusion.2
  664.1 0.3 bitcast_select_fusion.2
  664.3 0.1 copy.34
  664.4 0.4 fusion.12
  664.8 0.2 fusion.11
  665.0 61.8 %all-gather.4 = bf16[64,40,4]{1,2,0:T(4,128)(2,1)S(1)} all-gather(bf16[1,40,4]{1,2,0:T(4,128)(2,1)S(1)} %fusion.11), channel_id=1, replica_groups=mesh['sub'=64,'crs'=8] {'sub'}, dimensions={0}, use_global_device_ids=true | all-gather | bytes 20800 | tf_op jit(solution)/shard_map/all_gather | solution.py:102
  726.8 0.1 reshape.156
  727.0 0.5 fusion.7
  727.5 50.5 %all-reduce.1 = f32[320,4]{0,1:T(4,128)S(1)} all-reduce(f32[320,4]{0,1:T(4,128)S(1)} %fusion.7), channel_id=6, replica_groups=mesh['sub'=64,'crs'=8] {'crs'}, use_global_device_ids=true, to_apply=%region_7.9.clone | all-reduce | flops 1280 | bytes 10240
  778.0 0.2 fusion.61
  778.2 60.6 %all-gather.2 = bf16[4,24576]{1,0:T(4,128)(2,1)S(1)} all-gather(bf16[4,384]{1,0:T(4,128)(2,1)S(1)} %get-tuple-element.28), channel_id=4, replica_groups=mesh['sub'=64,'crs'=8] {'sub'}, dimensions={1}, use_global_device_ids=true | all-gather | bytes 199680 | tf_op jit(solution)/shard_map/all_gather | solution.py:71
  838.9 4.8 copy.36
  843.6 5.2 gather_fusion.3
  848.8 0.2 fusion.18
  849.0 0.0 copy-done.5
  849.0 0.7 multiply_reduce_fusion.2
  849.8 118.2 %psum.38 = f32[2,4]{1,0:T(2,128)S(1)} all-reduce(f32[2,4]{1,0:T(2,128)S(1)} %pad_maximum_fusion), channel_id=1, replica_groups=mesh['sub'=64,'crs'=8] {'sub','crs'}, use_global_device_ids=true, to_apply=%region_10.12 | all-reduce | flops 8 | bytes 64 | tf_op jit(solution)/shard_map/psum | solution.py:123
  967.9 0.2 multiply_reduce_fusion
  968.1 99.5 %psum.39 = f32[4]{0:T(128)S(1)} all-reduce(f32[4]{0:T(128)S(1)} %get-tuple-element.13), channel_id=1, replica_groups=mesh['sub'=64,'crs'=8] {'sub','crs'}, use_global_device_ids=true, to_apply=%region_12.14 | all-reduce | flops 4 | bytes 32 | tf_op jit(solution)/shard_map/psum | solution.py:128
  1067.6 0.1 divide_bitcast_fusion
  1067.7 0.6 copy.37
  1068.3 0.6 copy.38
  (13 shorter events, 0.1 us)
Async XLA Ops:
  0.6 247.8 %copy-start = (bf16[1,320,1,2560]{3,1,2,0:T(8,128)(2,1)S(1)}, bf16[1,320,1,2560]{3,1,2,0:T(8,128)(2,1)}, u32[]{:S(2)}) copy-start(bf16[1,320,1,2560]{3,1,2,0:T(8,128)(2,1)} %param.16) | copy-start | bytes 4915204
  0.6 185.7 %copy-start.4 = (f32[4,1,1,384]{3,2,1,0:T(1,128)S(1)}, f32[4,1,1,384]{3,2,1,0:T(1,128)}, u32[]{:S(2)}) copy-start(f32[4,1,1,384]{3,2,1,0:T(1,128)} %param.11) | copy-start | bytes 18436
  0.7 185.8 %copy-start.1 = (bf16[1,1,384,1152]{3,2,1,0:T(8,128)(2,1)S(1)}, bf16[1,1,384,1152]{3,2,1,0:T(8,128)(2,1)}, u32[]{:S(2)}) copy-start(bf16[1,1,384,1152]{3,2,1,0:T(8,128)(2,1)} %param.14) | copy-start | bytes 2654212
  0.7 186.3 %copy-start.3 = (f32[1,1,40,384]{3,2,1,0:T(8,128)S(1)}, f32[1,1,40,384]{3,2,1,0:T(8,128)}, u32[]{:S(2)}) copy-start(f32[1,1,40,384]{3,2,1,0:T(8,128)} %param.15) | copy-start | bytes 184324
  180.0 192.7 %copy-start.2 = (bf16[1,1,384,384]{3,2,1,0:T(8,128)(2,1)S(1)}, bf16[1,1,384,384]{3,2,1,0:T(8,128)(2,1)}, u32[]{:S(2)}) copy-start(bf16[1,1,384,384]{3,2,1,0:T(8,128)(2,1)} %param.12) | copy-start | bytes 884740
  664.8 184.2 %copy-start.5 = (bf16[1,1,384,768]{3,2,1,0:T(8,128)(2,1)S(1)}, bf16[1,1,384,768]{3,2,1,0:T(8,128)(2,1)}, u32[]{:S(2)}) copy-start(bf16[1,1,384,768]{3,2,1,0:T(8,128)(2,1)} %param.13) | copy-start | bytes 1769476
where the time goes:
time: 1070 us
  blocking collectives  1010 us (94%)
  local copies, waits for them, and re-layouts  43 us (4%)
    all_gather x4, blocking collectives, neighbour_rows(): lax.all_gather(vector_low.reshape(columns_count, 1, own_rows), 'sub', axi...  242 us
    psum x2, blocking collectives, body(): totals = lax.psum(local_terms, ('sub', 'crs')) / all_rows  237 us
    psum x2, blocking collectives, body(): lax.psum(jnp.sum(mapped * mapped, axis=1), ('sub', 'crs')) / all_rows  199 us
    all_gather x2, blocking collectives, body(): lax.all_gather(restricted_low, 'sub', axis=0, tiled=True)  123 us
    psum x1, blocking collectives, body(): lax.psum(jnp.sum(right_cols * right_cols, axis=1), ('sub', 'crs'))  111 us
    unnamed x2, blocking collectives  102 us

commit v1 on v0

v1 whole, which is shorter than its diff:
```python
import jax
import jax.numpy as jnp
from jax import lax
from jax.sharding import PartitionSpec as P

EPS = 1e-06
HIGH = lax.Precision.HIGHEST
LAST = (((1,), (1,)), ((), ()))


def least_squares(start_norm, columns):
    cosines = []
    sine_terms = []
    triangle = []
    target = [start_norm] + [jnp.zeros_like(start_norm) for j in range(len(columns))]
    for j, column in enumerate(columns):
        column = list(column)
        for i in range(j):
            upper_value = cosines[i] * column[i] + sine_terms[i] * column[i + 1]
            column[i + 1] = -sine_terms[i] * column[i] + cosines[i] * column[i + 1]
            column[i] = upper_value
        radius = jnp.sqrt(column[j] * column[j] + column[j + 1] * column[j + 1])
        cosine = column[j] / radius
        sine_part = column[j + 1] / radius
        column[j] = radius
        target[j + 1] = -sine_part * target[j]
        target[j] = cosine * target[j]
        cosines.append(cosine)
        sine_terms.append(sine_part)
        triangle.append(column[: j + 1])
    weights = [None] * len(columns)
    for j in reversed(range(len(columns))):
        running = target[j]
        for k in range(j + 1, len(columns)):
            running = running - triangle[k][j] * weights[k]
        weights[j] = running / triangle[j][j]
    return weights


def split3(x):
    hi = x.astype(jnp.bfloat16)
    rest = x - hi.astype(jnp.float32)
    mid = rest.astype(jnp.bfloat16)
    low = (rest - mid.astype(jnp.float32)).astype(jnp.bfloat16)
    return [hi, mid, low]


def body(
    right_side,
    own_block,
    coupling,
    local_inverse,
    coarse_basis,
    coarse_inverse,
    neighbours,
    margin_rows,
    block_counts,
):
    cols, own_rows = right_side.shape[0], right_side.shape[3]
    r = right_side.reshape(cols, own_rows)
    own_matrix = own_block[0, 0]
    couple_matrix = coupling[0, 0]
    inverse = local_inverse[0, 0]
    basis = coarse_basis[0, 0]
    kc = basis.shape[0]
    coarse_rows = coarse_inverse[0, :, 0, :]
    listed = neighbours[0, 0]
    picked = margin_rows[0, 0]
    live = block_counts[0, 0]
    slots, blk = picked.shape
    subs, owners = lax.axis_size("sub"), lax.axis_size("crs")
    all_rows = own_rows * subs * owners
    chosen = (listed[:, None] == jnp.arange(subs)[None, :]) & (
        jnp.arange(slots)[:, None] < live
    )
    chosen = chosen.astype(jnp.bfloat16)
    picks = (picked[:, :, None] == jnp.arange(own_rows)[None, None, :]).astype(jnp.bfloat16)

    def spread(block):
        copies = jnp.broadcast_to(block[None], (subs,) + block.shape)
        return lax.all_to_all(copies, "sub", 0, 0)

    def margin_of(gathered):
        near = jnp.einsum(
            "js,sqr->jqr", chosen, gathered, preferred_element_type=jnp.float32
        ).astype(jnp.bfloat16)
        rows = jnp.einsum(
            "jqr,jbr->qjb", near, picks, preferred_element_type=jnp.float32
        ).astype(jnp.bfloat16)
        return rows.reshape(cols, slots * blk)

    def restrict(v):
        return lax.dot_general(
            v, basis, LAST, precision=HIGH, preferred_element_type=jnp.float32
        ).astype(jnp.bfloat16)

    def precondition(v_low, gathered):
        margin = margin_of(gathered[:, :, :own_rows])
        fine = lax.dot_general(
            jnp.concatenate([v_low, margin], axis=1),
            inverse,
            LAST,
            preferred_element_type=jnp.float32,
        )
        coarse = gathered[:, :, own_rows : own_rows + kc]
        coarse = jnp.transpose(coarse, (1, 0, 2)).reshape(cols, subs * kc)
        share = lax.dot_general(coarse, coarse_rows, LAST, preferred_element_type=jnp.float32)
        return fine, share.reshape(cols, owners, kc).transpose(1, 0, 2)

    def operate(z_low, gathered):
        return lax.dot_general(
            z_low, own_matrix, LAST, preferred_element_type=jnp.float32
        ) + lax.dot_general(
            margin_of(gathered), couple_matrix, LAST, preferred_element_type=jnp.float32
        )

    def prolong(solved):
        return jnp.dot(solved, basis, precision=HIGH, preferred_element_type=jnp.float32)

    r_low = r.astype(jnp.bfloat16)
    fine, share = precondition(r_low, spread(jnp.concatenate([r_low, restrict(r)], axis=1)))
    solved = jnp.sum(lax.all_to_all(share, "crs", 0, 0), axis=0)
    p1 = fine + prolong(solved)
    p1_low = p1.astype(jnp.bfloat16)
    q1 = operate(p1_low, spread(p1_low))

    inner = jnp.stack(
        [jnp.sum(r * r, axis=1), jnp.sum(q1 * r, axis=1), jnp.sum(q1 * q1, axis=1)], axis=1
    )
    q1_low = q1.astype(jnp.bfloat16)
    gathered = spread(jnp.concatenate([q1_low, restrict(q1)] + split3(inner), axis=1))
    fine, share = precondition(q1_low, gathered)
    terms = gathered[:, :, own_rows + kc :].astype(jnp.float32)
    terms = jnp.sum(terms, axis=0).reshape(cols, 3, 3).sum(axis=1)
    share = jnp.concatenate([share, jnp.broadcast_to(terms[None], (owners, cols, 3))], axis=2)
    summed = jnp.sum(lax.all_to_all(share, "crs", 0, 0), axis=0)
    p2 = fine + prolong(summed[:, :kc])
    rr, qr, qq = [summed[:, kc + i] / all_rows for i in range(3)]

    start = jnp.sqrt(rr + EPS)
    h11 = qr / start / start
    w = q1 / start[:, None]
    v1 = r / start[:, None]
    part = h11 / start
    left = qq / start / start - 2.0 * part * (qr / start) + part * part * rr
    h21 = jnp.sqrt(jnp.maximum(left, 0.0) + EPS)
    v2 = (w - h11[:, None] * v1) / h21[:, None]
    z1 = p1 / start[:, None]
    z2 = (p2 / start[:, None] - h11[:, None] * z1) / h21[:, None]
    z2_low = z2.astype(jnp.bfloat16)
    w = operate(z2_low, spread(z2_low))
    pairs = [(w, v1), (w, v2), (w, w), (v1, v1), (v1, v2), (v2, v2)]
    inner = jnp.stack([jnp.sum(a * b, axis=1) for a, b in pairs])
    inner = lax.all_to_all(
        jnp.broadcast_to(inner[None], (owners,) + inner.shape), "crs", 0, 0
    ).sum(axis=0)
    inner = lax.all_to_all(
        jnp.broadcast_to(inner[None], (subs,) + inner.shape), "sub", 0, 0
    ).sum(axis=0)
    h12, h22, ww, g11, g12, g22 = inner / all_rows
    left = (
        ww
        - 2.0 * (h12 * h12 + h22 * h22)
        + h12 * h12 * g11
        + 2.0 * h12 * h22 * g12
        + h22 * h22 * g22
    )
    h32 = jnp.sqrt(jnp.maximum(left, 0.0) + EPS)
    v3 = (w - h12[:, None] * v1 - h22[:, None] * v2) / h32[:, None]
    weights = least_squares(start, [[h11, h21], [h12, h22, h32]])
    answer = weights[0][:, None] * z1 + weights[1][:, None] * z2
    shape = (cols, 1, 1, own_rows)
    return answer.reshape(shape), v3.reshape(shape)


def solution(mesh):
    in_specs = (
        P(None, "sub", "crs", None),
        P("sub", "crs", None, None),
        P("sub", "crs", None, None),
        P("sub", "crs", None, None),
        P("sub", "crs", None, None),
        P("sub", None, "crs", None),
        P("sub", "crs", None),
        P("sub", "crs", None, None),
        P("sub", "crs"),
    )
    out_specs = (P(None, "sub", "crs", None), P(None, "sub", "crs", None))
    return jax.shard_map(body, mesh=mesh, in_specs=in_specs, out_specs=out_specs, check_vma=False)
```

time: 1070 us -> 183 us (0.17)
  blocking collectives: 1010 us -> 54.1 us
  waiting for transfers between devices: 0 us -> 60.3 us
  starting transfers between devices: 0 us -> 45.6 us
  local copies, waits for them, and re-layouts: 43 us -> 8.54 us
    psum x5 -> x0, blocking collectives: 547 us -> none  [the longest x2 237 us: body(): totals = lax.psum(local_terms, ('sub', 'crs')) / all_rows]
    all_gather x6 -> x0, blocking collectives: 366 us -> none  [the longest x4 242 us: neighbour_rows(): lax.all_gather(vector_low.reshape(columns_count, 1, own_rows), 'sub', axi...]
    unnamed x2 -> x0, blocking collectives: 102 us -> none
    all_to_all x0 -> x5, waiting for transfers between devices: none -> 60.3 us  [the longest x3 52.4 us: spread(): return lax.all_to_all(copies, 'sub', 0, 0)]
    all_to_all x0 -> x3, blocking collectives: none -> 54.1 us  [the longest x1 25 us: spread(): return lax.all_to_all(copies, 'sub', 0, 0)]
    all_to_all x0 -> x5, starting transfers between devices: none -> 45.6 us  [the longest x3 28.4 us: spread(): return lax.all_to_all(copies, 'sub', 0, 0)]
    gather x4 -> x0, local copies, waits for them, and re-layouts: 20.8 us -> none  [neighbour_rows(): jnp.take(flattened, (listed[:, None] * own_rows + picked).reshape(-1), ax...]
    all_gather x6 -> x0, local copies, waits for them, and re-layouts: 19.1 us -> none  [the longest x4 19.1 us: neighbour_rows(): lax.all_gather(vector_low.reshape(columns_count, 1, own_rows), 'sub', axi...]
  transfers between devices with their start and end apart: 0 -> 5, of which waited for: 0 -> 5; matrix products, arithmetic and copies ran while one was open for 0% -> 1% of each run, Pallas kernels for 0% -> 0%
where the time goes in v1:
time: 183 us; the launch traced here: 181 us
  waiting for transfers between devices  60.3 us (33%)
  blocking collectives  54.1 us (30%)
  starting transfers between devices  45.6 us (25%)
  matrix products  8.64 us (5%)
  local copies, waits for them, and re-layouts  8.54 us (5%)
  other arithmetic  2.5 us (1%)
    all_to_all x3, waiting for transfers between devices, spread(): return lax.all_to_all(copies, 'sub', 0, 0)  52.4 us
    all_to_all x3, starting transfers between devices, spread(): return lax.all_to_all(copies, 'sub', 0, 0)  28.4 us
    all_to_all x1, blocking collectives, spread(): return lax.all_to_all(copies, 'sub', 0, 0)  25 us
    all_to_all x1, blocking collectives, body(): lax.all_to_all(jnp.broadcast_to(inner[None], (subs,) + inner.shape), 'sub...  18.7 us
    all_to_all x1, blocking collectives, body(): lax.all_to_all(jnp.broadcast_to(inner[None], (owners,) + inner.shape), 'c...  10.4 us
    all_to_all x1, starting transfers between devices, body(): solved = jnp.sum(lax.all_to_all(share, 'crs', 0, 0), axis=0)  8.67 us
    all_to_all x1, starting transfers between devices, body(): summed = jnp.sum(lax.all_to_all(share, 'crs', 0, 0), axis=0)  8.56 us
    unnamed x22, local copies, waits for them, and re-layouts  4.32 us
  transfers between devices with their start and end apart: 5, of which 5 were waited for; matrix products, arithmetic and copies ran while one was open for 1% of the time, Pallas kernels for 0%

profile of v1, /device:TPU:1, one launch (start us, length us, event | category | flops | bytes accessed | tf_op | source)
XLA Modules:
  0.0 181.2 jit_solution(1010520280044175398)
XLA Ops:
  0.6 0.8 copy.173
  1.5 1.0 convolution_convert_fusion.5
  2.5 0.8 broadcast_in_dim.14
  3.3 19.1 %all-to-all-start = ((bf16[64,4,424]{2,1,0:T(4,128)(2,1)}), bf16[64,4,424]{2,1,0:T(4,128)(2,1)S(1)}, u32[]{:S(2)}, u32[]{:S(2)}) async-start(bf16[64,4,424]{2,1,0:T(4,128)(2,1)} %broadcast_in_dim.14), calls=%async_computation | async-start | bytes 524288 | tf_op jit(solution)/shard_map/all_to_all | solution.py:81
  23.0 0.7 copy.174
  23.7 17.9 %all-to-all-done = bf16[64,4,424]{2,1,0:T(4,128)(2,1)S(1)} async-done(((bf16[64,4,424]{2,1,0:T(4,128)(2,1)}), bf16[64,4,424]{2,1,0:T(4,128)(2,1)S(1)}, u32[]{:S(2)}, u32[]{:S(2)}) %all-to-all-start) | async-done | bytes 217120 | tf_op jit(solution)/shard_map/all_to_all | solution.py:81
  41.7 0.1 reshape.200
  41.8 1.0 convolution_bitcast_fusion.1
  42.8 0.7 reshape.215
  43.5 8.7 %all-to-all-start.1 = ((f32[8,1,160]{2,1,0:T(1,128)}), f32[8,1,160]{2,1,0:T(1,128)S(1)}, u32[]{:S(2)}, u32[]{:S(2)}) async-start(f32[8,1,160]{2,1,0:T(1,128)} %reshape.215), calls=%async_computation.1 | async-start | bytes 16384 | tf_op jit(solution)/shard_map/all_to_all | solution.py:122
  52.3 0.2 convolution_convert_fusion.3
  52.5 0.4 fusion.11
  52.9 0.3 fusion.17
  53.2 3.6 %all-to-all-done.1 = f32[8,1,160]{2,1,0:T(1,128)S(1)} async-done(((f32[8,1,160]{2,1,0:T(1,128)}), f32[8,1,160]{2,1,0:T(1,128)S(1)}, u32[]{:S(2)}, u32[]{:S(2)}) %all-to-all-start.1) | async-done | bytes 5152 | tf_op jit(solution)/shard_map/all_to_all | solution.py:122
  56.8 0.5 broadcast.171
  57.3 0.7 reduce.22
  58.0 0.1 reshape.216
  58.1 0.2 fusion.90
  58.2 0.7 broadcast_in_dim.15
  59.0 4.7 %all-to-all-start.2 = ((bf16[64,4,384]{2,1,0:T(4,128)(2,1)}), bf16[64,4,384]{2,1,0:T(4,128)(2,1)S(1)}, u32[]{:S(2)}, u32[]{:S(2)}) async-start(bf16[64,4,384]{2,1,0:T(4,128)(2,1)} %broadcast_in_dim.15), calls=%async_computation.2 | async-start | bytes 393216 | tf_op jit(solution)/shard_map/all_to_all | solution.py:81
  63.7 0.2 fusion.29
  63.9 16.8 %all-to-all-done.2 = bf16[64,4,384]{2,1,0:T(4,128)(2,1)S(1)} async-done(((bf16[64,4,384]{2,1,0:T(4,128)(2,1)}), bf16[64,4,384]{2,1,0:T(4,128)(2,1)S(1)}, u32[]{:S(2)}, u32[]{:S(2)}) %all-to-all-start.2) | async-done | bytes 196640 | tf_op jit(solution)/shard_map/all_to_all | solution.py:81
  80.6 0.2 convolution_convert_fusion.2
  80.8 1.8 fusion.52
  82.6 0.1 copy.112
  82.7 0.1 copy.113
  82.8 0.1 copy.114
  82.9 0.1 subtract_convert_fusion
  83.0 0.2 convolution_convert_fusion.4
  83.2 0.1 concatenate.17
  83.3 0.1 broadcast_in_dim.16
  83.4 25.0 %all_to_all.40 = bf16[64,4,433]{2,1,0:T(4,128)(2,1)S(1)} all-to-all(bf16[64,4,433]{2,1,0:T(4,128)(2,1)S(1)} %broadcast_in_dim.16), channel_id=1, replica_groups=mesh['sub'=64,'crs'=8] {'sub'}, dimensions={0} | all-to-all | bytes 443392 | tf_op jit(solution)/shard_map/all_to_all | solution.py:81
  108.3 0.1 slice.40
  108.4 0.2 convolution_convert_fusion.1
  108.6 0.4 fusion.9
  109.1 0.1 reshape.201
  109.2 1.0 convolution_bitcast_fusion
  110.2 0.2 convert_reduce_fusion
  110.4 0.1 reshape.194
  110.5 0.1 pad_maximum_fusion
  110.6 0.7 reshape.217
  111.3 8.6 %all-to-all-start.4 = ((f32[8,1,172]{2,1,0:T(1,128)}), f32[8,1,172]{2,1,0:T(1,128)S(1)}, u32[]{:S(2)}, u32[]{:S(2)}) async-start(f32[8,1,172]{2,1,0:T(1,128)} %reshape.217), calls=%async_computation.4 | async-start | bytes 16384 | tf_op jit(solution)/shard_map/all_to_all | solution.py:136
  119.8 0.3 fusion.15
  120.2 4.3 %all-to-all-done.4 = f32[8,1,172]{2,1,0:T(1,128)S(1)} async-done(((f32[8,1,172]{2,1,0:T(1,128)}), f32[8,1,172]{2,1,0:T(1,128)S(1)}, u32[]{:S(2)}, u32[]{:S(2)}) %all-to-all-start.4) | async-done | bytes 5536 | tf_op jit(solution)/shard_map/all_to_all | solution.py:136
  124.5 0.7 reduce.23
  125.1 0.1 reshape.218
  125.2 0.2 fusion.88
  125.5 0.2 fusion.93
  125.6 0.7 broadcast_in_dim.18
  126.4 4.6 %all-to-all-start.5 = ((bf16[64,4,384]{2,1,0:T(4,128)(2,1)}), bf16[64,4,384]{2,1,0:T(4,128)(2,1)S(1)}, u32[]{:S(2)}, u32[]{:S(2)}) async-start(bf16[64,4,384]{2,1,0:T(4,128)(2,1)} %broadcast_in_dim.18), calls=%async_computation.5 | async-start | bytes 393216 | tf_op jit(solution)/shard_map/all_to_all | solution.py:81
  131.0 0.2 fusion.27
  131.2 17.8 %all-to-all-done.5 = bf16[64,4,384]{2,1,0:T(4,128)(2,1)S(1)} async-done(((bf16[64,4,384]{2,1,0:T(4,128)(2,1)}), bf16[64,4,384]{2,1,0:T(4,128)(2,1)S(1)}, u32[]{:S(2)}, u32[]{:S(2)}) %all-to-all-start.5) | async-done | bytes 196640 | tf_op jit(solution)/shard_map/all_to_all | solution.py:81
  149.0 0.2 convolution_convert_fusion
  149.2 0.7 multiply_reduce_fusion
  149.9 0.1 copy.120
  150.0 10.4 %all_to_all.41 = f32[8,6,4]{1,2,0:T(4,128)S(1)} all-to-all(f32[8,6,4]{1,2,0:T(4,128)S(1)} %broadcast_in_dim.19), channel_id=1, replica_groups=mesh['sub'=64,'crs'=8] {'crs'}, dimensions={0} | all-to-all | bytes 1536 | tf_op jit(solution)/shard_map/all_to_all | solution.py:154
  160.5 18.7 %all_to_all.42 = f32[64,6,4]{1,2,0:T(4,128)S(1)} all-to-all(f32[64,6,4]{1,2,0:T(4,128)S(1)} %broadcast_in_dim.20), channel_id=1, replica_groups=mesh['sub'=64,'crs'=8] {'sub'}, dimensions={0} | all-to-all | bytes 12288 | tf_op jit(solution)/shard_map/all_to_all | solution.py:157
  179.2 0.1 reduce_sum.149
  179.3 0.3 slice_reduce_fusion.3
  179.5 0.1 divide_bitcast_fusion
  179.6 0.6 copy.136
  180.2 0.2 fusion.77
  180.5 0.1 add_bitcast_fusion
  180.5 0.6 copy.135
  (32 shorter events, 0.4 us)
Async XLA Ops:
  0.6 41.2 %copy-start = (bf16[1,320,1,2560]{3,1,2,0:T(8,128)(2,1)S(1)}, bf16[1,320,1,2560]{3,1,2,0:T(8,128)(2,1)}, u32[]{:S(2)}) copy-start(bf16[1,320,1,2560]{3,1,2,0:T(8,128)(2,1)} %param.14) | copy-start | bytes 4915204
  3.3 38.3 %all-to-all-start = ((bf16[64,4,424]{2,1,0:T(4,128)(2,1)}), bf16[64,4,424]{2,1,0:T(4,128)(2,1)S(1)}, u32[]{:S(2)}, u32[]{:S(2)}) async-start(bf16[64,4,424]{2,1,0:T(4,128)(2,1)} %broadcast_in_dim.14), calls=%async_computation | async-start | bytes 524288 | tf_op jit(solution)/shard_map/all_to_all | solution.py:81
  41.6 10.6 %copy-start.6 = (s32[1,1,6]{2,1,0:T(1,128)S(1)}, s32[1,1,6]{2,1,0:T(1,128)}, u32[]{:S(2)}) copy-start(s32[1,1,6]{2,1,0:T(1,128)} %param.15) | copy-start | bytes 76
  41.8 11.1 %copy-start.1 = (bf16[1,1,384,1152]{3,2,1,0:T(8,128)(2,1)S(1)}, bf16[1,1,384,1152]{3,2,1,0:T(8,128)(2,1)}, u32[]{:S(2)}) copy-start(bf16[1,1,384,1152]{3,2,1,0:T(8,128)(2,1)} %param.12) | copy-start | bytes 2654212
  42.8 15.3 %copy-start.3 = (f32[1,1,40,384]{3,2,1,0:T(8,128)S(1)}, f32[1,1,40,384]{3,2,1,0:T(8,128)}, u32[]{:S(2)}) copy-start(f32[1,1,40,384]{3,2,1,0:T(8,128)} %param.13) | copy-start | bytes 184324
  43.5 13.3 %all-to-all-start.1 = ((f32[8,1,160]{2,1,0:T(1,128)}), f32[8,1,160]{2,1,0:T(1,128)S(1)}, u32[]{:S(2)}, u32[]{:S(2)}) async-start(f32[8,1,160]{2,1,0:T(1,128)} %reshape.215), calls=%async_computation.1 | async-start | bytes 16384 | tf_op jit(solution)/shard_map/all_to_all | solution.py:122
  52.3 11.4 %copy-start.2 = (bf16[1,1,384,384]{3,2,1,0:T(8,128)(2,1)S(1)}, bf16[1,1,384,384]{3,2,1,0:T(8,128)(2,1)}, u32[]{:S(2)}) copy-start(bf16[1,1,384,384]{3,2,1,0:T(8,128)(2,1)} %param.10) | copy-start | bytes 884740
  52.9 28.0 %copy-start.4 = (f32[4,1,1,384]{3,2,1,0:T(1,128)S(1)}, f32[4,1,1,384]{3,2,1,0:T(1,128)}, u32[]{:S(2)}) copy-start(f32[4,1,1,384]{3,2,1,0:T(1,128)} %param.9) | copy-start | bytes 18436
  59.0 21.7 %all-to-all-start.2 = ((bf16[64,4,384]{2,1,0:T(4,128)(2,1)}), bf16[64,4,384]{2,1,0:T(4,128)(2,1)S(1)}, u32[]{:S(2)}, u32[]{:S(2)}) async-start(bf16[64,4,384]{2,1,0:T(4,128)(2,1)} %broadcast_in_dim.15), calls=%async_computation.2 | async-start | bytes 393216 | tf_op jit(solution)/shard_map/all_to_all | solution.py:81
  110.6 38.6 %copy-start.5 = (bf16[1,1,384,768]{3,2,1,0:T(8,128)(2,1)S(1)}, bf16[1,1,384,768]{3,2,1,0:T(8,128)(2,1)}, u32[]{:S(2)}) copy-start(bf16[1,1,384,768]{3,2,1,0:T(8,128)(2,1)} %param.11) | copy-start | bytes 1769476
  111.3 13.2 %all-to-all-start.4 = ((f32[8,1,172]{2,1,0:T(1,128)}), f32[8,1,172]{2,1,0:T(1,128)S(1)}, u32[]{:S(2)}, u32[]{:S(2)}) async-start(f32[8,1,172]{2,1,0:T(1,128)} %reshape.217), calls=%async_computation.4 | async-start | bytes 16384 | tf_op jit(solution)/shard_map/all_to_all | solution.py:136
  126.4 22.6 %all-to-all-start.5 = ((bf16[64,4,384]{2,1,0:T(4,128)(2,1)}), bf16[64,4,384]{2,1,0:T(4,128)(2,1)S(1)}, u32[]{:S(2)}, u32[]{:S(2)}) async-start(bf16[64,4,384]{2,1,0:T(4,128)(2,1)} %broadcast_in_dim.18), calls=%async_computation.5 | async-start | bytes 393216 | tf_op jit(solution)/shard_map/all_to_all | solution.py:81

commit v2 on v0

v2 whole, which is shorter than its diff:
```python
import jax
import jax.numpy as jnp
from jax import lax
from jax.experimental import pallas as pl
from jax.experimental.pallas import tpu as pltpu
from jax.sharding import PartitionSpec as P

EPS = 1e-06
HIGH = lax.Precision.HIGHEST
LAST = (((1,), (1,)), ((), ()))
FIRST = (((1,), (0,)), ((), ()))
LANES = 128
VMEM_BYTES = 16 << 20


def least_squares(start_norm, columns):
    cosines = []
    sine_terms = []
    triangle = []
    target = [start_norm] + [jnp.zeros_like(start_norm) for j in range(len(columns))]
    for j, column in enumerate(columns):
        column = list(column)
        for i in range(j):
            upper_value = cosines[i] * column[i] + sine_terms[i] * column[i + 1]
            column[i + 1] = -sine_terms[i] * column[i] + cosines[i] * column[i + 1]
            column[i] = upper_value
        radius = jnp.sqrt(column[j] * column[j] + column[j + 1] * column[j + 1])
        cosine = column[j] / radius
        sine_part = column[j + 1] / radius
        column[j] = radius
        target[j + 1] = -sine_part * target[j]
        target[j] = cosine * target[j]
        cosines.append(cosine)
        sine_terms.append(sine_part)
        triangle.append(column[: j + 1])
    weights = [None] * len(columns)
    for j in reversed(range(len(columns))):
        running = target[j]
        for k in range(j + 1, len(columns)):
            running = running - triangle[k][j] * weights[k]
        weights[j] = running / triangle[j][j]
    return weights


def split3(x):
    hi = x.astype(jnp.bfloat16).astype(jnp.float32)
    rest = x - hi
    mid = rest.astype(jnp.bfloat16).astype(jnp.float32)
    return hi, mid, rest - mid


def place(column, lane, at):
    return jnp.where(lane == at, column, 0.0)


def pick_lanes(tiles, index):
    low = index & (LANES - 1)
    high = index >> 7
    out = jnp.take_along_axis(tiles[0], low, axis=1, mode="promise_in_bounds")
    for t in range(1, len(tiles)):
        other = jnp.take_along_axis(tiles[t], low, axis=1, mode="promise_in_bounds")
        out = jnp.where(high == t, other, out)
    return out


def lanes_of(shape):
    return lax.broadcasted_iota(jnp.int32, shape, 1)


def twice(x):
    return jnp.concatenate([x, x], axis=0)


def send_rows(vector, asked_ref, out_ref):
    tiles = [twice(vector[:, t * LANES : (t + 1) * LANES]) for t in range(vector.shape[1] // LANES)]
    cols = vector.shape[0]
    for i in range(asked_ref.shape[0]):
        chosen = pick_lanes(tiles, asked_ref[i])
        out_ref[2 * i, :, 0:LANES] = chosen[:cols].astype(jnp.bfloat16)
        out_ref[2 * i + 1, :, 0:LANES] = chosen[cols:].astype(jnp.bfloat16)


def margin_from(got_ref, near_ref, live_ref, slots):
    parts = []
    for j in range(slots):
        part = got_ref[near_ref[j], :, 0:LANES]
        parts.append(jnp.where(j < live_ref[0], part, jnp.zeros_like(part)))
    return jnp.concatenate(parts, axis=1)


def first_send_kernel(near_ref, live_ref, r_ref, basis_ref, picked_ref, out_ref):
    subs, cols, _ = out_ref.shape
    rows = r_ref.shape[1]
    kc = basis_ref.shape[0]
    r = r_ref[...]
    low = r.astype(jnp.bfloat16)
    residual = lax.dot_general(
        r, basis_ref[...], LAST, precision=HIGH, preferred_element_type=jnp.float32
    )
    tail = jnp.concatenate([residual, jnp.zeros((cols, LANES - kc), jnp.float32)], axis=1)
    whole = jnp.concatenate([low, tail.astype(jnp.bfloat16)], axis=1)
    out_ref[...] = jnp.broadcast_to(whole[None], out_ref.shape)
    lane = lanes_of((cols, LANES))
    sub = lax.broadcasted_iota(jnp.int32, (cols, LANES), 0)
    wide = LANES // cols
    slots = picked_ref.shape[0]
    for j in range(slots):
        wanted = (picked_ref[pl.ds(j, 1), :] - rows // 2).astype(jnp.float32)
        wanted = jnp.broadcast_to(wanted, (cols, LANES))
        packed = jnp.zeros((cols, LANES), jnp.float32)
        for i in range(cols):
            moved = pltpu.roll(wanted, (kc - i * wide) % LANES, 1)
            packed = jnp.where(sub == i, moved, packed)
        packed = jnp.where((lane >= kc) & (lane < kc + wide), packed, tail)

        @pl.when(j < live_ref[0])
        def _():
            out_ref[near_ref[j], :, rows : rows + LANES] = packed.astype(jnp.bfloat16)


def share_kernel(at, with_terms, got_ref, coarse_ref, out_ref):
    subs, cols, _ = got_ref.shape
    owners = out_ref.shape[0]
    kc = coarse_ref.shape[0] // owners
    lane = lanes_of((cols, LANES))
    tiles = [jnp.zeros((cols, LANES), jnp.float32) for _ in range(subs * kc // LANES)]
    terms = jnp.zeros((cols, LANES), jnp.float32)
    for s in range(subs):
        got = got_ref[s, :, at : at + LANES].astype(jnp.float32)
        if with_terms:
            terms = terms + got
        t, off = divmod(s * kc, LANES)
        moved = pltpu.roll(got, off, 1) if off else got
        if off + kc <= LANES:
            tiles[t] = jnp.where((lane >= off) & (lane < off + kc), moved, tiles[t])
        else:
            tiles[t] = jnp.where(lane >= off, moved, tiles[t])
            tiles[t + 1] = jnp.where(lane < off + kc - LANES, moved, tiles[t + 1])
    residuals = jnp.concatenate(tiles, axis=1).astype(jnp.bfloat16)
    share = lax.dot_general(
        residuals, coarse_ref[...], LAST, preferred_element_type=jnp.float32
    )
    extra = jnp.zeros((cols, LANES), jnp.float32)
    if with_terms:
        summed = terms + pltpu.roll(terms, LANES - 3, 1) + pltpu.roll(terms, LANES - 6, 1)
        extra = jnp.where((lane >= kc) & (lane < kc + 3), summed, 0.0)
    wide = jnp.concatenate(
        [share, jnp.zeros((cols, -share.shape[1] % LANES), jnp.float32)], axis=1
    )
    for c in range(owners):
        t, off = divmod(c * kc, LANES)
        part = wide[:, t * LANES : (t + 1) * LANES]
        if off:
            part = pltpu.roll(part, LANES - off, 1)
        if off + kc > LANES:
            after = pltpu.roll(wide[:, (t + 1) * LANES : (t + 2) * LANES], LANES - off, 1)
            part = jnp.where(lane < LANES - off, part, after)
        out_ref[c] = jnp.where(lane < kc, part, extra)


def first_fine_kernel(
    kc, near_ref, live_ref, r_ref, picked_ref, got_ref, inverse_ref, fine_ref, asked_ref
):
    subs, cols, _ = got_ref.shape
    rows = r_ref.shape[1]
    slots = picked_ref.shape[0]
    parts = [r_ref[...].astype(jnp.bfloat16)]
    for j in range(slots):
        near = got_ref[near_ref[j], :, 0:rows].astype(jnp.float32)
        tiles = [twice(near[:, t * LANES : (t + 1) * LANES]) for t in range(rows // LANES)]
        index = jnp.broadcast_to(picked_ref[pl.ds(j, 1), :], (2 * cols, LANES))
        part = pick_lanes(tiles, index)[:cols]
        parts.append(jnp.where(j < live_ref[0], part, 0.0).astype(jnp.bfloat16))
    extended = jnp.concatenate(parts, axis=1)
    fine_ref[...] = lax.dot_general(
        extended, inverse_ref[...], LAST, preferred_element_type=jnp.float32
    )
    lane = lanes_of((cols, LANES))
    wide = LANES // cols
    for i in range(subs // 2):
        pair = []
        for s in (2 * i, 2 * i + 1):
            got = got_ref[s, :, rows : rows + LANES].astype(jnp.float32)
            index = jnp.zeros((cols, LANES), jnp.float32)
            for k in range(cols):
                moved = pltpu.roll(
                    jnp.broadcast_to(got[k : k + 1], (cols, LANES)), (k * wide - kc) % LANES, 1
                )
                index = jnp.where((lane >= k * wide) & (lane < (k + 1) * wide), moved, index)
            pair.append(index)
        index = jnp.concatenate(pair, axis=0).astype(jnp.int32) + rows // 2
        asked_ref[i] = jnp.clip(index, 0, rows - 1)


def fine_kernel(near_ref, live_ref, vector_ref, got_ref, inverse_ref, fine_ref):
    rows = vector_ref.shape[1]
    slots = (inverse_ref.shape[1] - rows) // LANES
    margin = margin_from(got_ref, near_ref, live_ref, slots)
    extended = jnp.concatenate([vector_ref[...].astype(jnp.bfloat16), margin], axis=1)
    fine_ref[...] = lax.dot_general(
        extended, inverse_ref[...], LAST, preferred_element_type=jnp.float32
    )


def prolong(summed, fine_ref, basis_ref):
    kc = basis_ref.shape[0]
    return fine_ref[...] + lax.dot_general(
        summed[:, :kc], basis_ref[...], FIRST, precision=HIGH, preferred_element_type=jnp.float32
    )


def first_direction_kernel(shares_ref, fine_ref, basis_ref, asked_ref, p_ref, out_ref):
    p = prolong(jnp.sum(shares_ref[...], axis=0), fine_ref, basis_ref)
    p_ref[...] = p
    send_rows(p, asked_ref, out_ref)


def own_kernel(vector_ref, own_ref, out_ref):
    out_ref[...] = lax.dot_general(
        vector_ref[...].astype(jnp.bfloat16), own_ref[...], LAST, preferred_element_type=jnp.float32
    )


def operate(near_ref, live_ref, own_part_ref, got_ref, coupling_ref):
    margin = margin_from(got_ref, near_ref, live_ref, coupling_ref.shape[1] // LANES)
    return own_part_ref[...] + lax.dot_general(
        margin, coupling_ref[...], LAST, preferred_element_type=jnp.float32
    )


def row_sum(x):
    return jnp.sum(x, axis=1, keepdims=True)


def first_operate_kernel(
    near_ref, live_ref, own_part_ref, got_ref, coupling_ref, r_ref, basis_ref, asked_ref, q_ref, out_ref
):
    cols = r_ref.shape[0]
    kc = basis_ref.shape[0]
    q = operate(near_ref, live_ref, own_part_ref, got_ref, coupling_ref)
    q_ref[...] = q
    r = r_ref[...]
    residual = lax.dot_general(
        q, basis_ref[...], LAST, precision=HIGH, preferred_element_type=jnp.float32
    )
    tail = jnp.concatenate([residual, jnp.zeros((cols, LANES - kc), jnp.float32)], axis=1)
    lane = lanes_of((cols, LANES))
    for i, inner in enumerate([row_sum(r * r), row_sum(q * r), row_sum(q * q)]):
        for k, term in enumerate(split3(inner)):
            tail = jnp.where(lane == kc + 3 * k + i, term, tail)
    send_rows(q, asked_ref, out_ref)
    out_ref[:, :, LANES : 2 * LANES] = jnp.broadcast_to(
        tail.astype(jnp.bfloat16)[None], (out_ref.shape[0], cols, LANES)
    )


def second_direction_kernel(
    all_rows, shares_ref, fine_ref, basis_ref, asked_ref, r_ref, q_ref, p_ref,
    v1_ref, v2_ref, z1_ref, z2_ref, scalars_ref, out_ref,
):
    kc = basis_ref.shape[0]
    summed = jnp.sum(shares_ref[...], axis=0)
    p2 = prolong(summed, fine_ref, basis_ref)
    rr, qr, qq = [summed[:, kc + i : kc + i + 1] / all_rows for i in range(3)]
    start = jnp.sqrt(rr + EPS)
    h11 = qr / start / start
    part = h11 / start
    left = qq / start / start - 2.0 * part * (qr / start) + part * part * rr
    h21 = jnp.sqrt(jnp.maximum(left, 0.0) + EPS)
    v1 = r_ref[...] / start
    z1 = p_ref[...] / start
    v2 = (q_ref[...] / start - h11 * v1) / h21
    z2 = (p2 / start - h11 * z1) / h21
    v1_ref[...] = v1
    v2_ref[...] = v2
    z1_ref[...] = z1
    z2_ref[...] = z2
    lane = lanes_of(scalars_ref.shape)
    scalars_ref[...] = place(start, lane, 0) + place(h11, lane, 1) + place(h21, lane, 2)
    send_rows(z2, asked_ref, out_ref)


def second_operate_kernel(
    near_ref, live_ref, own_part_ref, got_ref, coupling_ref, v1_ref, v2_ref, w_ref, out_ref
):
    w = operate(near_ref, live_ref, own_part_ref, got_ref, coupling_ref)
    w_ref[...] = w
    v1 = v1_ref[...]
    v2 = v2_ref[...]
    lane = lanes_of((w.shape[0], LANES))
    pairs = [(w, v1), (w, v2), (w, w), (v1, v1), (v1, v2), (v2, v2)]
    inner = jnp.zeros((w.shape[0], LANES), jnp.float32)
    for i, (a, b) in enumerate(pairs):
        inner = inner + place(row_sum(a * b), lane, i)
    out_ref[...] = jnp.broadcast_to(inner[None], out_ref.shape)


def between_kernel(got_ref, out_ref):
    out_ref[...] = jnp.broadcast_to(jnp.sum(got_ref[...], axis=0)[None], out_ref.shape)


def last_kernel(
    all_rows, got_ref, w_ref, v1_ref, v2_ref, z1_ref, z2_ref, scalars_ref, answer_ref, next_ref
):
    inner = jnp.sum(got_ref[...], axis=0) / all_rows
    h12, h22, ww, g11, g12, g22 = [inner[:, i : i + 1] for i in range(6)]
    start, h11, h21 = [scalars_ref[:, i : i + 1] for i in range(3)]
    left = (
        ww
        - 2.0 * (h12 * h12 + h22 * h22)
        + h12 * h12 * g11
        + 2.0 * h12 * h22 * g12
        + h22 * h22 * g22
    )
    h32 = jnp.sqrt(jnp.maximum(left, 0.0) + EPS)
    next_ref[...] = (w_ref[...] - h12 * v1_ref[...] - h22 * v2_ref[...]) / h32
    weights = least_squares(start, [[h11, h21], [h12, h22, h32]])
    answer_ref[...] = weights[0] * z1_ref[...] + weights[1] * z2_ref[...]


def call(kernel, outs, *args, scalars=0, name):
    smem = pl.BlockSpec(memory_space=pltpu.SMEM)
    vmem = pl.BlockSpec(memory_space=pltpu.VMEM)
    return pl.pallas_call(
        kernel,
        out_shape=outs,
        in_specs=[smem] * scalars + [vmem] * (len(args) - scalars),
        out_specs=jax.tree.map(lambda _: vmem, outs),
        compiler_params=pltpu.CompilerParams(vmem_limit_bytes=VMEM_BYTES),
        name=name,
    )(*args)


def body(
    right_side,
    own_block,
    coupling,
    local_inverse,
    coarse_basis,
    coarse_inverse,
    neighbours,
    margin_rows,
    block_counts,
):
    cols, rows = right_side.shape[0], right_side.shape[3]
    r = right_side.reshape(cols, rows)
    own = own_block[0, 0]
    couple = coupling[0, 0]
    inverse = local_inverse[0, 0]
    basis = coarse_basis[0, 0]
    coarse = coarse_inverse[0, :, 0, :]
    near = neighbours[0, 0]
    picked = margin_rows[0, 0]
    live = block_counts[0]
    subs, owners = lax.axis_size("sub"), lax.axis_size("crs")
    all_rows = rows * subs * owners
    f32, bf16 = jnp.float32, jnp.bfloat16

    def shape(*dims, dtype=f32):
        return jax.ShapeDtypeStruct(dims, dtype)

    vector = shape(cols, rows)
    tile = shape(cols, LANES)

    def over_sub(blocks):
        return lax.all_to_all(blocks, "sub", 0, 0)

    def over_crs(blocks):
        return lax.all_to_all(blocks, "crs", 0, 0)

    def share_of(at, with_terms, got, name):
        def kernel(*refs):
            share_kernel(at, with_terms, *refs)

        return call(kernel, shape(owners, cols, LANES), got, coarse, name=name)

    sent = call(
        first_send_kernel, shape(subs, cols, rows + LANES, dtype=bf16),
        near, live, r, basis, picked, scalars=2, name="first_send",
    )
    got = over_sub(sent)
    shares = over_crs(share_of(rows, False, got, "first_share"))

    def first_fine(*refs):
        first_fine_kernel(basis.shape[0], *refs)

    fine, asked = call(
        first_fine, (vector, shape(subs // 2, 2 * cols, LANES, dtype=jnp.int32)),
        near, live, r, picked, got, inverse, scalars=2, name="first_fine",
    )
    p1, sent = call(
        first_direction_kernel, (vector, shape(subs, cols, LANES, dtype=bf16)),
        shares, fine, basis, asked, name="first_direction",
    )
    got = over_sub(sent)
    own_part = call(own_kernel, vector, p1, own, name="first_own")
    q1, sent = call(
        first_operate_kernel, (vector, shape(subs, cols, 2 * LANES, dtype=bf16)),
        near, live, own_part, got, couple, r, basis, asked, scalars=2, name="first_operate",
    )
    got = over_sub(sent)
    shares = over_crs(share_of(LANES, True, got, "second_share"))
    fine = call(
        fine_kernel, vector, near, live, q1, got, inverse, scalars=2, name="second_fine"
    )

    def second_direction(*refs):
        second_direction_kernel(float(all_rows), *refs)

    v1, v2, z1, z2, scalars, sent = call(
        second_direction,
        (vector, vector, vector, vector, tile, shape(subs, cols, LANES, dtype=bf16)),
        shares, fine, basis, asked, r, q1, p1, name="second_direction",
    )
    got = over_sub(sent)
    own_part = call(own_kernel, vector, z2, own, name="second_own")
    w, sent = call(
        second_operate_kernel, (vector, shape(owners, cols, LANES)),
        near, live, own_part, got, couple, v1, v2, scalars=2, name="second_operate",
    )
    got = over_crs(sent)
    sent = call(between_kernel, shape(subs, cols, LANES), got, name="between")
    got = over_sub(sent)

    def last(*refs):
        last_kernel(float(all_rows), *refs)

    answer, following = call(
        last, (vector, vector), got, w, v1, v2, z1, z2, scalars, name="last"
    )
    out = (cols, 1, 1, rows)
    return answer.reshape(out), following.reshape(out)


def solution(mesh):
    in_specs = (
        P(None, "sub", "crs", None),
        P("sub", "crs", None, None),
        P("sub", "crs", None, None),
        P("sub", "crs", None, None),
        P("sub", "crs", None, None),
        P("sub", None, "crs", None),
        P("sub", "crs", None),
        P("sub", "crs", None, None),
        P("sub", "crs"),
    )
    out_specs = (P(None, "sub", "crs", None), P(None, "sub", "crs", None))
    return jax.shard_map(body, mesh=mesh, in_specs=in_specs, out_specs=out_specs, check_vma=False)
```

time: 1070 us -> 169 us (0.16)
  blocking collectives: 1010 us -> 85.7 us
  waiting for transfers between devices: 0 us -> 33.5 us
  local copies, waits for them, and re-layouts: 43 us -> 11.8 us
  starting transfers between devices: 0 us -> 25 us
    psum x5 -> x0, blocking collectives: 547 us -> none  [the longest x2 237 us: body(): totals = lax.psum(local_terms, ('sub', 'crs')) / all_rows]
    all_gather x6 -> x0, blocking collectives: 366 us -> none  [the longest x4 242 us: neighbour_rows(): lax.all_gather(vector_low.reshape(columns_count, 1, own_rows), 'sub', axi...]
    unnamed x2 -> x0, blocking collectives: 102 us -> none
    all_to_all x0 -> x4, blocking collectives: none -> 85.7 us  [the longest x3 76.5 us: over_sub(): return lax.all_to_all(blocks, 'sub', 0, 0)]
    all_to_all x0 -> x4, waiting for transfers between devices: none -> 33.5 us  [the longest x2 26.6 us: over_sub(): return lax.all_to_all(blocks, 'sub', 0, 0)]
    all_to_all x0 -> x4, starting transfers between devices: none -> 25 us  [the longest x2 15.7 us: over_crs(): return lax.all_to_all(blocks, 'crs', 0, 0)]
    gather x4 -> x0, local copies, waits for them, and re-layouts: 20.8 us -> none  [neighbour_rows(): jnp.take(flattened, (listed[:, None] * own_rows + picked).reshape(-1), ax...]
    all_gather x6 -> x0, local copies, waits for them, and re-layouts: 19.1 us -> none  [the longest x4 19.1 us: neighbour_rows(): lax.all_gather(vector_low.reshape(columns_count, 1, own_rows), 'sub', axi...]
  transfers between devices with their start and end apart: 0 -> 4, of which waited for: 0 -> 4; matrix products, arithmetic and copies ran while one was open for 0% -> 0% of each run, Pallas kernels for 0% -> 1%
where the time goes in v2:
time: 169 us; the launch traced here: 167 us
  blocking collectives  85.7 us (51%)
  waiting for transfers between devices  33.5 us (20%)
  starting transfers between devices  25 us (15%)
  local copies, waits for them, and re-layouts  11.8 us (7%)
  Pallas kernels  9.59 us (6%)
    all_to_all x3, blocking collectives, over_sub(): return lax.all_to_all(blocks, 'sub', 0, 0)  76.5 us
    all_to_all x2, waiting for transfers between devices, over_sub(): return lax.all_to_all(blocks, 'sub', 0, 0)  26.6 us
    all_to_all x2, starting transfers between devices, over_crs(): return lax.all_to_all(blocks, 'crs', 0, 0)  15.7 us
    unnamed x42, local copies, waits for them, and re-layouts  11.8 us
    pallas_call x13, Pallas kernels, call(): pl.pallas_call(kernel, out_shape=outs, in_specs=[smem] * scalars + [vmem]...  9.59 us
    all_to_all x2, starting transfers between devices, over_sub(): return lax.all_to_all(blocks, 'sub', 0, 0)  9.25 us
    all_to_all x1, blocking collectives, over_crs(): return lax.all_to_all(blocks, 'crs', 0, 0)  9.21 us
    all_to_all x2, waiting for transfers between devices, over_crs(): return lax.all_to_all(blocks, 'crs', 0, 0)  6.86 us
  transfers between devices with their start and end apart: 4, of which 4 were waited for; matrix products, arithmetic and copies ran while one was open for 0% of the time, Pallas kernels for 1%

profile of v2, /device:TPU:1, one launch (start us, length us, event | category | flops | bytes accessed | tf_op | source)
XLA Modules:
  0.0 167.1 jit_solution(14059512548799397920)
XLA Ops:
  0.6 0.0 copy-start.2
  1.4 0.7 copy.18
  2.1 0.7 copy.17
  2.7 0.0 copy-start.8
  2.7 0.8 copy-done.8
  3.6 0.7 copy-done.15
  4.2 0.0 copy-start.16
  4.2 1.1 first_send.1
  5.3 38.1 %all_to_all.40.refs_0_.refs_4_ = bf16[64,4,512]{2,1,0:T(4,128)(2,1)S(1)} all-to-all(bf16[64,4,512]{2,1,0:T(4,128)(2,1)S(1)} %first_send.1), channel_id=1, replica_groups=mesh['sub'=64,'crs'=8] {'sub'}, dimensions={0} | all-to-all | bytes 524288 | tf_op jit(solution)/shard_map/all_to_all | solution.py:366
  43.5 0.0 copy-start
  43.5 1.4 copy-done
  44.9 0.0 copy-start.3
  44.9 1.2 first_share.1
  46.1 0.0 copy-start.1
  46.1 8.8 %all-to-all-start.1 = ((f32[8,4,128]{2,1,0:T(4,128)}), f32[8,4,128]{2,1,0:T(4,128)S(1)}, u32[]{:S(2)}, u32[]{:S(2)}) async-start(f32[8,4,128]{2,1,0:T(4,128)} %first_share.1), calls=%async_computation.1 | async-start | bytes 32768 | tf_op jit(solution)/shard_map/all_to_all | solution.py:369
  54.9 0.0 copy-done.2
  54.9 0.0 copy-done.16
  54.9 0.9 first_fine.1
  55.9 0.0 copy-start.6
  55.9 3.7 %all-to-all-done.1.shares_ref = f32[8,4,128]{2,1,0:T(4,128)S(1)} async-done(((f32[8,4,128]{2,1,0:T(4,128)}), f32[8,4,128]{2,1,0:T(4,128)S(1)}, u32[]{:S(2)}, u32[]{:S(2)}) %all-to-all-start.1) | async-done | bytes 16416 | tf_op jit(solution)/shard_map/all_to_all | solution.py:369
  59.6 0.0 copy-start.9
  59.6 0.8 copy-done.9
  60.4 1.0 first_direction.1
  61.4 0.0 copy-start.13
  61.4 4.7 %all-to-all-start.2 = ((bf16[64,4,128]{2,1,0:T(4,128)(2,1)}), bf16[64,4,128]{2,1,0:T(4,128)(2,1)S(1)}, u32[]{:S(2)}, u32[]{:S(2)}) async-start(bf16[64,4,128]{2,1,0:T(4,128)(2,1)} %get-tuple-element.21), calls=%async_computation.2 | async-start | bytes 131072 | tf_op jit(solution)/shard_map/all_to_all | solution.py:366
  66.1 0.0 copy-start.4
  66.1 1.0 copy-done.4
  67.1 0.2 first_own.1.own_part_ref
  67.3 12.8 %all-to-all-done.2.got_ref = bf16[64,4,128]{2,1,0:T(4,128)(2,1)S(1)} async-done(((bf16[64,4,128]{2,1,0:T(4,128)(2,1)}), bf16[64,4,128]{2,1,0:T(4,128)(2,1)S(1)}, u32[]{:S(2)}, u32[]{:S(2)}) %all-to-all-start.2) | async-done | bytes 65568 | tf_op jit(solution)/shard_map/all_to_all | solution.py:366
  80.1 0.0 copy-done.3
  80.1 0.0 copy-start.10
  80.1 0.8 copy-done.10
  80.9 1.1 first_operate.1
  82.0 0.0 copy-done.6
  82.1 0.0 copy-done.13
  82.1 19.0 %all_to_all.41.refs_0_.got_ref = bf16[64,4,256]{2,1,0:T(4,128)(2,1)S(1)} all-to-all(bf16[64,4,256]{2,1,0:T(4,128)(2,1)S(1)} %get-tuple-element.22), channel_id=1, replica_groups=mesh['sub'=64,'crs'=8] {'sub'}, dimensions={0} | all-to-all | bytes 262144 | tf_op jit(solution)/shard_map/all_to_all | solution.py:366
  101.1 0.0 copy-done.1
  101.1 0.0 copy-start.5
  101.1 0.6 second_share.1
  101.7 0.0 copy-start.12
  101.7 0.6 copy-done.12
  102.3 0.0 copy-start.18
  102.3 6.9 %all-to-all-start.4 = ((f32[8,4,128]{2,1,0:T(4,128)}), f32[8,4,128]{2,1,0:T(4,128)S(1)}, u32[]{:S(2)}, u32[]{:S(2)}) async-start(f32[8,4,128]{2,1,0:T(4,128)} %copy-done.12), calls=%async_computation.4 | async-start | bytes 32768 | tf_op jit(solution)/shard_map/all_to_all | solution.py:369
  109.2 0.0 copy-start.17
  109.2 0.7 copy-done.17
  109.9 0.9 second_fine.1.refs_1_
  110.7 3.2 %all-to-all-done.4.refs_0_ = f32[8,4,128]{2,1,0:T(4,128)S(1)} async-done(((f32[8,4,128]{2,1,0:T(4,128)}), f32[8,4,128]{2,1,0:T(4,128)S(1)}, u32[]{:S(2)}, u32[]{:S(2)}) %all-to-all-start.4) | async-done | bytes 16416 | tf_op jit(solution)/shard_map/all_to_all | solution.py:369
  113.9 0.9 copy-done.7
  114.8 0.0 copy-start.11
  114.8 0.8 copy-done.11
  115.6 0.0 copy-start.14
  115.6 0.7 copy-done.14
  116.3 1.1 second_direction.1
  117.4 4.6 %all-to-all-start.5 = ((bf16[64,4,128]{2,1,0:T(4,128)(2,1)}), bf16[64,4,128]{2,1,0:T(4,128)(2,1)S(1)}, u32[]{:S(2)}, u32[]{:S(2)}) async-start(bf16[64,4,128]{2,1,0:T(4,128)(2,1)} %get-tuple-element.25), calls=%async_computation.5 | async-start | bytes 131072 | tf_op jit(solution)/shard_map/all_to_all | solution.py:366
  122.0 0.0 copy-done.5
  122.0 0.2 second_own.1.own_part_ref
  122.2 13.8 %all-to-all-done.5.got_ref = bf16[64,4,128]{2,1,0:T(4,128)(2,1)S(1)} async-done(((bf16[64,4,128]{2,1,0:T(4,128)(2,1)}), bf16[64,4,128]{2,1,0:T(4,128)(2,1)S(1)}, u32[]{:S(2)}, u32[]{:S(2)}) %all-to-all-start.5) | async-done | bytes 65568 | tf_op jit(solution)/shard_map/all_to_all | solution.py:366
  136.0 0.0 copy-done.18
  136.0 0.9 second_operate.1
  136.9 9.2 %all_to_all.42.got_ref = f32[8,4,128]{2,1,0:T(4,128)S(1)} all-to-all(f32[8,4,128]{2,1,0:T(4,128)S(1)} %get-tuple-element.28), channel_id=1, replica_groups=mesh['sub'=64,'crs'=8] {'crs'}, dimensions={0} | all-to-all | bytes 32768 | tf_op jit(solution)/shard_map/all_to_all | solution.py:369
  146.1 19.4 %all_to_all.43.refs_0_ = f32[64,4,128]{2,1,0:T(4,128)S(1)} all-to-all(f32[64,4,128]{2,1,0:T(4,128)S(1)} %between.1), channel_id=1, replica_groups=mesh['sub'=64,'crs'=8] {'sub'}, dimensions={0} | all-to-all | bytes 262144 | tf_op jit(solution)/shard_map/all_to_all | solution.py:366
  165.5 0.4 last.1
  165.9 0.6 copy.11
  166.5 0.6 copy.12
  (3 shorter events, 0.0 us)
Async XLA Ops:
  0.6 54.3 %copy-start.2 = (bf16[1,1,384,1152]{3,2,1,0:T(8,128)(2,1)S(1)}, bf16[1,1,384,1152]{3,2,1,0:T(8,128)(2,1)}, u32[]{:S(2)}) copy-start(bf16[1,1,384,1152]{3,2,1,0:T(8,128)(2,1)} %param.12) | copy-start | bytes 2654212
  2.7 0.8 copy-start.8
  3.6 0.7 copy-start.15
  4.2 50.7 %copy-start.16 = (s32[1,1,6]{2,1,0:T(1,128)S(1)}, s32[1,1,6]{2,1,0:T(1,128)}, u32[]{:S(2)}) copy-start(s32[1,1,6]{2,1,0:T(1,128)} %param.15) | copy-start | bytes 76
  43.5 1.4 copy-start
  44.9 35.2 %copy-start.3 = (bf16[1,1,384,768]{3,2,1,0:T(8,128)(2,1)S(1)}, bf16[1,1,384,768]{3,2,1,0:T(8,128)(2,1)}, u32[]{:S(2)}) copy-start(bf16[1,1,384,768]{3,2,1,0:T(8,128)(2,1)} %param.11) | copy-start | bytes 1769476
  46.1 54.9 %copy-start.1 = (bf16[1,320,1,2560]{3,1,2,0:T(8,128)(2,1)S(1)}, bf16[1,320,1,2560]{3,1,2,0:T(8,128)(2,1)}, u32[]{:S(2)}) copy-start(bf16[1,320,1,2560]{3,1,2,0:T(8,128)(2,1)} %param.14) | copy-start | bytes 4915204
  46.1 13.5 %all-to-all-start.1 = ((f32[8,4,128]{2,1,0:T(4,128)}), f32[8,4,128]{2,1,0:T(4,128)S(1)}, u32[]{:S(2)}, u32[]{:S(2)}) async-start(f32[8,4,128]{2,1,0:T(4,128)} %first_share.1), calls=%async_computation.1 | async-start | bytes 32768 | tf_op jit(solution)/shard_map/all_to_all | solution.py:369
  55.9 26.2 %copy-start.6 = (s32[32,8,128]{2,1,0:T(8,128)}, s32[32,8,128]{2,1,0:T(8,128)S(1)}, u32[]{:S(2)}) copy-start(s32[32,8,128]{2,1,0:T(8,128)S(1)} %get-tuple-element.19.asked_ref.refs_3_) | copy-start | bytes 393220
  59.6 0.8 copy-start.9
  61.4 20.6 %copy-start.13 = (f32[4,384]{1,0:T(4,128)}, f32[4,384]{1,0:T(4,128)S(1)}, u32[]{:S(2)}) copy-start(f32[4,384]{1,0:T(4,128)S(1)} %get-tuple-element.20.vector_ref.refs_6_) | copy-start | bytes 18436
  61.4 18.7 %all-to-all-start.2 = ((bf16[64,4,128]{2,1,0:T(4,128)(2,1)}), bf16[64,4,128]{2,1,0:T(4,128)(2,1)S(1)}, u32[]{:S(2)}, u32[]{:S(2)}) async-start(bf16[64,4,128]{2,1,0:T(4,128)(2,1)} %get-tuple-element.21), calls=%async_computation.2 | async-start | bytes 131072 | tf_op jit(solution)/shard_map/all_to_all | solution.py:366
  66.1 1.0 copy-start.4
  80.1 0.8 copy-start.10
  101.1 21.0 %copy-start.5 = (bf16[1,1,384,384]{3,2,1,0:T(8,128)(2,1)S(1)}, bf16[1,1,384,384]{3,2,1,0:T(8,128)(2,1)}, u32[]{:S(2)}) copy-start(bf16[1,1,384,384]{3,2,1,0:T(8,128)(2,1)} %param.10) | copy-start | bytes 884740
  101.7 0.6 copy-start.12
  102.3 33.7 %copy-start.18 = (s32[1,1,6]{2,1,0:T(1,128)S(1)}, s32[1,1,6]{2,1,0:T(1,128)}, u32[]{:S(2)}) copy-start(s32[1,1,6]{2,1,0:T(1,128)} %param.15) | copy-start | bytes 76
  102.3 11.6 %all-to-all-start.4 = ((f32[8,4,128]{2,1,0:T(4,128)}), f32[8,4,128]{2,1,0:T(4,128)S(1)}, u32[]{:S(2)}, u32[]{:S(2)}) async-start(f32[8,4,128]{2,1,0:T(4,128)} %copy-done.12), calls=%async_computation.4 | async-start | bytes 32768 | tf_op jit(solution)/shard_map/all_to_all | solution.py:369
  109.2 0.7 copy-start.17
  113.9 0.9 copy-start.7
  114.8 0.8 copy-start.11
  115.6 0.7 copy-start.14
  117.4 18.6 %all-to-all-start.5 = ((bf16[64,4,128]{2,1,0:T(4,128)(2,1)}), bf16[64,4,128]{2,1,0:T(4,128)(2,1)S(1)}, u32[]{:S(2)}, u32[]{:S(2)}) async-start(bf16[64,4,128]{2,1,0:T(4,128)(2,1)} %get-tuple-element.25), calls=%async_computation.5 | async-start | bytes 131072 | tf_op jit(solution)/shard_map/all_to_all | solution.py:366

commit v3 on v2

--- a/solution.py
+++ b/solution.py
@@ -88,11 +88,31 @@
     return jnp.concatenate(parts, axis=1)
 
 
-def first_send_kernel(near_ref, live_ref, r_ref, basis_ref, picked_ref, out_ref):
+def first_send_kernel(
+    near, live, r_hbm, basis_hbm, picked_hbm, coarse_hbm, inverse_hbm, own_hbm, couple_hbm,
+    out_ref, r_ref, basis_ref, picked, coarse_ref, inverse_ref, own_ref, couple_ref, sems,
+):
+    pairs = [
+        (r_hbm, r_ref),
+        (basis_hbm, basis_ref),
+        (picked_hbm, picked),
+        (coarse_hbm, coarse_ref),
+        (inverse_hbm, inverse_ref),
+        (own_hbm, own_ref),
+        (couple_hbm, couple_ref),
+    ]
+    moves = [
+        pltpu.make_async_copy(source, target, sems.at[i])
+        for i, (source, target) in enumerate(pairs)
+    ]
+    for move in moves:
+        move.start()
+    for move in moves[:3]:
+        move.wait()
     subs, cols, _ = out_ref.shape
-    rows = r_ref.shape[1]
+    rows = r_ref.shape[2]
     kc = basis_ref.shape[0]
-    r = r_ref[...]
+    r = r_ref[:, 0, :]
     low = r.astype(jnp.bfloat16)
     residual = lax.dot_general(
         r, basis_ref[...], LAST, precision=HIGH, preferred_element_type=jnp.float32
@@ -103,9 +123,9 @@
     lane = lanes_of((cols, LANES))
     sub = lax.broadcasted_iota(jnp.int32, (cols, LANES), 0)
     wide = LANES // cols
-    slots = picked_ref.shape[0]
+    slots = picked.shape[0]
     for j in range(slots):
-        wanted = (picked_ref[pl.ds(j, 1), :] - rows // 2).astype(jnp.float32)
+        wanted = (picked[j] - rows // 2).astype(jnp.float32)
         wanted = jnp.broadcast_to(wanted, (cols, LANES))
         packed = jnp.zeros((cols, LANES), jnp.float32)
         for i in range(cols):
@@ -113,12 +133,15 @@
             packed = jnp.where(sub == i, moved, packed)
         packed = jnp.where((lane >= kc) & (lane < kc + wide), packed, tail)
 
-        @pl.when(j < live_ref[0])
+        @pl.when(j < live[0])
         def _():
-            out_ref[near_ref[j], :, rows : rows + LANES] = packed.astype(jnp.bfloat16)
-
-
-def share_kernel(at, with_terms, got_ref, coarse_ref, out_ref):
+            out_ref[near[j], :, rows : rows + LANES] = packed.astype(jnp.bfloat16)
+
+    for move in moves[3:]:
+        move.wait()
+
+
+def write_share(at, with_terms, got_ref, coarse_ref, out_ref):
     subs, cols, _ = got_ref.shape
     owners = out_ref.shape[0]
     kc = coarse_ref.shape[0] // owners
@@ -158,17 +181,18 @@
         out_ref[c] = jnp.where(lane < kc, part, extra)
 
 
-def first_fine_kernel(
-    kc, near_ref, live_ref, r_ref, picked_ref, got_ref, inverse_ref, fine_ref, asked_ref
+def first_gather_kernel(
+    near_ref, live_ref, r_ref, picked_ref, got_ref, inverse_ref, coarse_ref, fine_ref, asked_ref, out_ref
 ):
     subs, cols, _ = got_ref.shape
-    rows = r_ref.shape[1]
+    rows = r_ref.shape[2]
     slots = picked_ref.shape[0]
-    parts = [r_ref[...].astype(jnp.bfloat16)]
+    write_share(rows, False, got_ref, coarse_ref, out_ref)
+    parts = [r_ref[:, 0, :].astype(jnp.bfloat16)]
     for j in range(slots):
         near = got_ref[near_ref[j], :, 0:rows].astype(jnp.float32)
         tiles = [twice(near[:, t * LANES : (t + 1) * LANES]) for t in range(rows // LANES)]
-        index = jnp.broadcast_to(picked_ref[pl.ds(j, 1), :], (2 * cols, LANES))
+        index = jnp.broadcast_to(picked_ref[j], (2 * cols, LANES))
         part = pick_lanes(tiles, index)[:cols]
         parts.append(jnp.where(j < live_ref[0], part, 0.0).astype(jnp.bfloat16))
     extended = jnp.concatenate(parts, axis=1)
@@ -176,6 +200,7 @@
         extended, inverse_ref[...], LAST, preferred_element_type=jnp.float32
     )
     lane = lanes_of((cols, LANES))
+    kc = coarse_ref.shape[0] // out_ref.shape[0]
     wide = LANES // cols
     for i in range(subs // 2):
         pair = []
@@ -192,9 +217,12 @@
         asked_ref[i] = jnp.clip(index, 0, rows - 1)
 
 
-def fine_kernel(near_ref, live_ref, vector_ref, got_ref, inverse_ref, fine_ref):
+def second_gather_kernel(
+    near_ref, live_ref, vector_ref, got_ref, inverse_ref, coarse_ref, fine_ref, out_ref
+):
     rows = vector_ref.shape[1]
     slots = (inverse_ref.shape[1] - rows) // LANES
+    write_share(LANES, True, got_ref, coarse_ref, out_ref)
     margin = margin_from(got_ref, near_ref, live_ref, slots)
     extended = jnp.concatenate([vector_ref[...].astype(jnp.bfloat16), margin], axis=1)
     fine_ref[...] = lax.dot_general(
@@ -215,17 +243,12 @@
     send_rows(p, asked_ref, out_ref)
 
 
-def own_kernel(vector_ref, own_ref, out_ref):
-    out_ref[...] = lax.dot_general(
-        vector_ref[...].astype(jnp.bfloat16), own_ref[...], LAST, preferred_element_type=jnp.float32
-    )
-
-
-def operate(near_ref, live_ref, own_part_ref, got_ref, coupling_ref):
+def operate(near_ref, live_ref, vector_ref, got_ref, own_ref, coupling_ref):
     margin = margin_from(got_ref, near_ref, live_ref, coupling_ref.shape[1] // LANES)
-    return own_part_ref[...] + lax.dot_general(
-        margin, coupling_ref[...], LAST, preferred_element_type=jnp.float32
-    )
+    low = vector_ref[...].astype(jnp.bfloat16)
+    return lax.dot_general(
+        low, own_ref[...], LAST, preferred_element_type=jnp.float32
+    ) + lax.dot_general(margin, coupling_ref[...], LAST, preferred_element_type=jnp.float32)
 
 
 def row_sum(x):
@@ -233,13 +256,13 @@
 
 
 def first_operate_kernel(
-    near_ref, live_ref, own_part_ref, got_ref, coupling_ref, r_ref, basis_ref, asked_ref, q_ref, out_ref
+    near_ref, live_ref, p_ref, got_ref, own_ref, coupling_ref, r_ref, basis_ref, asked_ref, q_ref, out_ref
 ):
     cols = r_ref.shape[0]
     kc = basis_ref.shape[0]
-    q = operate(near_ref, live_ref, own_part_ref, got_ref, coupling_ref)
+    q = operate(near_ref, live_ref, p_ref, got_ref, own_ref, coupling_ref)
     q_ref[...] = q
-    r = r_ref[...]
+    r = r_ref[:, 0, :]
     residual = lax.dot_general(
         q, basis_ref[...], LAST, precision=HIGH, preferred_element_type=jnp.float32
     )
@@ -267,7 +290,7 @@
     part = h11 / start
     left = qq / start / start - 2.0 * part * (qr / start) + part * part * rr
     h21 = jnp.sqrt(jnp.maximum(left, 0.0) + EPS)
-    v1 = r_ref[...] / start
+    v1 = r_ref[:, 0, :] / start
     z1 = p_ref[...] / start
     v2 = (q_ref[...] / start - h11 * v1) / h21
     z2 = (p2 / start - h11 * z1) / h21
@@ -281,18 +304,20 @@
 
 
 def second_operate_kernel(
-    near_ref, live_ref, own_part_ref, got_ref, coupling_ref, v1_ref, v2_ref, w_ref, out_ref
-):
-    w = operate(near_ref, live_ref, own_part_ref, got_ref, coupling_ref)
+    near_ref, live_ref, z_ref, got_ref, own_ref, coupling_ref, v1_ref, v2_ref, w_ref, out_ref
+):
+    w = operate(near_ref, live_ref, z_ref, got_ref, own_ref, coupling_ref)
     w_ref[...] = w
     v1 = v1_ref[...]
     v2 = v2_ref[...]
-    lane = lanes_of((w.shape[0], LANES))
+    cols = w.shape[0]
+    lane = lanes_of((cols, LANES))
+    col = lax.broadcasted_iota(jnp.int32, (cols, LANES), 0)
     pairs = [(w, v1), (w, v2), (w, w), (v1, v1), (v1, v2), (v2, v2)]
-    inner = jnp.zeros((w.shape[0], LANES), jnp.float32)
+    inner = jnp.zeros((cols, LANES), jnp.float32)
     for i, (a, b) in enumerate(pairs):
-        inner = inner + place(row_sum(a * b), lane, i)
-    out_ref[...] = jnp.broadcast_to(inner[None], out_ref.shape)
+        inner = jnp.where(lane == i * cols + col, row_sum(a * b), inner)
+    out_ref[...] = jnp.broadcast_to(jnp.sum(inner, axis=0, keepdims=True)[None], out_ref.shape)
 
 
 def between_kernel(got_ref, out_ref):
@@ -302,8 +327,13 @@
 def last_kernel(
     all_rows, got_ref, w_ref, v1_ref, v2_ref, z1_ref, z2_ref, scalars_ref, answer_ref, next_ref
 ):
-    inner = jnp.sum(got_ref[...], axis=0) / all_rows
-    h12, h22, ww, g11, g12, g22 = [inner[:, i : i + 1] for i in range(6)]
+    cols = w_ref.shape[0]
+    lane = lanes_of((cols, LANES))
+    col = lax.broadcasted_iota(jnp.int32, (cols, LANES), 0)
+    inner = jnp.broadcast_to(jnp.sum(got_ref[...], axis=0) / all_rows, (cols, LANES))
+    h12, h22, ww, g11, g12, g22 = [
+        row_sum(jnp.where(lane == i * cols + col, inner, 0.0)) for i in range(6)
+    ]
     start, h11, h21 = [scalars_ref[:, i : i + 1] for i in range(3)]
     left = (
         ww
@@ -313,9 +343,9 @@
         + h22 * h22 * g22
     )
     h32 = jnp.sqrt(jnp.maximum(left, 0.0) + EPS)
-    next_ref[...] = (w_ref[...] - h12 * v1_ref[...] - h22 * v2_ref[...]) / h32
+    next_ref[:, 0, :] = (w_ref[...] - h12 * v1_ref[...] - h22 * v2_ref[...]) / h32
     weights = least_squares(start, [[h11, h21], [h12, h22, h32]])
-    answer_ref[...] = weights[0] * z1_ref[...] + weights[1] * z2_ref[...]
+    answer_ref[:, 0, :] = weights[0] * z1_ref[...] + weights[1] * z2_ref[...]
 
 
 def call(kernel, outs, *args, scalars=0, name):
@@ -343,14 +373,14 @@
     block_counts,
 ):
     cols, rows = right_side.shape[0], right_side.shape[3]
-    r = right_side.reshape(cols, rows)
+    r = right_side.reshape(cols, 1, rows)
     own = own_block[0, 0]
     couple = coupling[0, 0]
     inverse = local_inverse[0, 0]
     basis = coarse_basis[0, 0]
     coarse = coarse_inverse[0, :, 0, :]
     near = neighbours[0, 0]
-    picked = margin_rows[0, 0]
+    picked = margin_rows.reshape(margin_rows.shape[2], 1, margin_rows.shape[3])
     live = block_counts[0]
     subs, owners = lax.axis_size("sub"), lax.axis_size("crs")
     all_rows = rows * subs * owners
@@ -368,41 +398,44 @@
     def over_crs(blocks):
         return lax.all_to_all(blocks, "crs", 0, 0)
 
-    def share_of(at, with_terms, got, name):
-        def kernel(*refs):
-            share_kernel(at, with_terms, *refs)
-
-        return call(kernel, shape(owners, cols, LANES), got, coarse, name=name)
-
-    sent = call(
-        first_send_kernel, shape(subs, cols, rows + LANES, dtype=bf16),
-        near, live, r, basis, picked, scalars=2, name="first_send",
-    )
+    near_live = (near, live)
+    held = [r, basis, picked, coarse, inverse, own, couple]
+    vmem = pl.BlockSpec(memory_space=pltpu.VMEM)
+    sent, r, basis, picked, coarse, inverse, own, couple = pl.pallas_call(
+        first_send_kernel,
+        out_shape=[shape(subs, cols, rows + LANES, dtype=bf16)]
+        + [shape(*x.shape, dtype=x.dtype) for x in held],
+        in_specs=[pl.BlockSpec(memory_space=pltpu.SMEM)] * 2
+        + [pl.BlockSpec(memory_space=pltpu.HBM)] * 7,
+        out_specs=[vmem] * 8,
+        scratch_shapes=[
+            pltpu.SemaphoreType.DMA((7,)),
+        ],
+        compiler_params=pltpu.CompilerParams(vmem_limit_bytes=VMEM_BYTES),
+        name="first_send",
+    )(near, live, *[pltpu.with_memory_space_constraint(x, pltpu.HBM) for x in held])
     got = over_sub(sent)
-    shares = over_crs(share_of(rows, False, got, "first_share"))
-
-    def first_fine(*refs):
-        first_fine_kernel(basis.shape[0], *refs)
-
-    fine, asked = call(
-        first_fine, (vector, shape(subs // 2, 2 * cols, LANES, dtype=jnp.int32)),
-        near, live, r, picked, got, inverse, scalars=2, name="first_fine",
-    )
+    fine, asked, shares = call(
+        first_gather_kernel,
+        (vector, shape(subs // 2, 2 * cols, LANES, dtype=jnp.int32), shape(owners, cols, LANES)),
+        *near_live, r, picked, got, inverse, coarse, scalars=2, name="first_gather",
+    )
+    shares = over_crs(shares)
     p1, sent = call(
         first_direction_kernel, (vector, shape(subs, cols, LANES, dtype=bf16)),
         shares, fine, basis, asked, name="first_direction",
     )
     got = over_sub(sent)
-    own_part = call(own_kernel, vector, p1, own, name="first_own")
     q1, sent = call(
         first_operate_kernel, (vector, shape(subs, cols, 2 * LANES, dtype=bf16)),
-        near, live, own_part, got, couple, r, basis, asked, scalars=2, name="first_operate",
+        *near_live, p1, got, own, couple, r, basis, asked, scalars=2, name="first_operate",
     )
     got = over_sub(sent)
-    shares = over_crs(share_of(LANES, True, got, "second_share"))
-    fine = call(
-        fine_kernel, vector, near, live, q1, got, inverse, scalars=2, name="second_fine"
-    )
+    fine, shares = call(
+        second_gather_kernel, (vector, shape(owners, cols, LANES)),
+        *near_live, q1, got, inverse, coarse, scalars=2, name="second_gather",
+    )
+    shares = over_crs(shares)
 
     def second_direction(*refs):
         second_direction_kernel(float(all_rows), *refs)
@@ -413,20 +446,20 @@
         shares, fine, basis, asked, r, q1, p1, name="second_direction",
     )
     got = over_sub(sent)
-    own_part = call(own_kernel, vector, z2, own, name="second_own")
     w, sent = call(
-        second_operate_kernel, (vector, shape(owners, cols, LANES)),
-        near, live, own_part, got, couple, v1, v2, scalars=2, name="second_operate",
+        second_operate_kernel, (vector, shape(owners, 1, LANES)),
+        *near_live, z2, got, own, couple, v1, v2, scalars=2, name="second_operate",
     )
     got = over_crs(sent)
-    sent = call(between_kernel, shape(subs, cols, LANES), got, name="between")
+    sent = call(between_kernel, shape(subs, 1, LANES), got, name="between")
     got = over_sub(sent)
 
     def last(*refs):
         last_kernel(float(all_rows), *refs)
 
     answer, following = call(
-        last, (vector, vector), got, w, v1, v2, z1, z2, scalars, name="last"
+        last, (shape(cols, 1, rows), shape(cols, 1, rows)),
+        got, w, v1, v2, z1, z2, scalars, name="last",
     )
     out = (cols, 1, 1, rows)
     return answer.reshape(out), following.reshape(out)

time: 169 us -> 155 us (0.917); the launches traced: 167 us -> 155 us
  blocking collectives: 85.7 us -> 144 us
  waiting for transfers between devices: 33.5 us -> 0 us
  starting transfers between devices: 25 us -> 0 us
  local copies, waits for them, and re-layouts: 11.8 us -> 0.66 us
    all_to_all x3 -> x5, blocking collectives: 76.5 us -> 111 us  [over_sub(): return lax.all_to_all(blocks, 'sub', 0, 0)]
    all_to_all x4 -> x0, waiting for transfers between devices: 33.5 us -> none  [the longest x2 26.6 us: over_sub(): return lax.all_to_all(blocks, 'sub', 0, 0)]
    all_to_all x4 -> x0, starting transfers between devices: 25 us -> none  [the longest x2 15.7 us: over_crs(): return lax.all_to_all(blocks, 'crs', 0, 0)]
    all_to_all x1 -> x3, blocking collectives: 9.21 us -> 32.8 us  [over_crs(): return lax.all_to_all(blocks, 'crs', 0, 0)]
    unnamed x42 -> x4, local copies, waits for them, and re-layouts: 11.8 us -> 0.66 us
    pallas_call x13 -> x8, Pallas kernels: 9.59 us -> 6.9 us  [call(): pl.pallas_call(kernel, out_shape=outs, in_specs=[smem] * scalars + [vmem]...]
    pallas_call x0 -> x1, Pallas kernels: none -> 2.58 us  [body(): pl.pallas_call(first_send_kernel, out_shape=[shape(subs, cols, rows + LAN...]
  transfers between devices with their start and end apart: 4 -> 0, of which waited for: 4 -> 0; matrix products, arithmetic and copies ran while one was open for 0% -> 0% of each run, Pallas kernels for 1% -> 0%
where the time goes in v3:
time: 155 us
  blocking collectives  144 us (93%)
  Pallas kernels  9.48 us (6%)
    all_to_all x5, blocking collectives, over_sub(): return lax.all_to_all(blocks, 'sub', 0, 0)  111 us
    all_to_all x3, blocking collectives, over_crs(): return lax.all_to_all(blocks, 'crs', 0, 0)  32.8 us
    pallas_call x8, Pallas kernels, call(): pl.pallas_call(kernel, out_shape=outs, in_specs=[smem] * scalars + [vmem]...  6.9 us

profile of v3, /device:TPU:1, one launch (start us, length us, event | category | flops | bytes accessed | tf_op | source)
XLA Modules:
  0.0 155.0 jit_solution(370056514775420851)
XLA Ops:
  1.3 0.0 copy-start
  1.3 0.6 copy-done
  1.9 2.6 %first_send.1 = (bf16[64,4,512]{2,1,0:T(4,128)(2,1)S(1)}, f32[4,1,384]{2,1,0:T(1,128)S(1)}, f32[40,384]{1,0:T(8,128)S(1)}, s32[6,1,128]{2,1,0:T(1,128)S(1)}, bf1...) custom-call(s32[6]{0:T(128)S(1)} %bitcast.20, ...), custom_call_target="tpu_custom_call" | custom-call | tf_op jit(solution)/shard_map/first_send/pallas_call | solution.py:404
  4.5 38.1 %all_to_all.40.got_ref = bf16[64,4,512]{2,1,0:T(4,128)(2,1)S(1)} all-to-all(bf16[64,4,512]{2,1,0:T(4,128)(2,1)S(1)} %get-tuple-element.31), channel_id=1, replica_groups=mesh['sub'=64,'crs'=8] {'sub'}, dimensions={0} | all-to-all | bytes 524288 | tf_op jit(solution)/shard_map/all_to_all | solution.py:396
  42.6 1.4 first_gather.1
  44.1 13.1 %all_to_all.41.shares_ref = f32[8,4,128]{2,1,0:T(4,128)S(1)} all-to-all(f32[8,4,128]{2,1,0:T(4,128)S(1)} %get-tuple-element.34), channel_id=1, replica_groups=mesh['sub'=64,'crs'=8] {'crs'}, dimensions={0} | all-to-all | bytes 32768 | tf_op jit(solution)/shard_map/all_to_all | solution.py:399
  57.2 0.4 first_direction.1
  57.6 18.5 %all_to_all.42.got_ref = bf16[64,4,128]{2,1,0:T(4,128)(2,1)S(1)} all-to-all(bf16[64,4,128]{2,1,0:T(4,128)(2,1)S(1)} %get-tuple-element.39), channel_id=1, replica_groups=mesh['sub'=64,'crs'=8] {'sub'}, dimensions={0} | all-to-all | bytes 131072 | tf_op jit(solution)/shard_map/all_to_all | solution.py:396
  76.1 1.2 first_operate.1
  77.3 0.0 copy-start.1
  77.3 18.9 %all_to_all.43.got_ref = bf16[64,4,256]{2,1,0:T(4,128)(2,1)S(1)} all-to-all(bf16[64,4,256]{2,1,0:T(4,128)(2,1)S(1)} %get-tuple-element.43), channel_id=1, replica_groups=mesh['sub'=64,'crs'=8] {'sub'}, dimensions={0} | all-to-all | bytes 262144 | tf_op jit(solution)/shard_map/all_to_all | solution.py:396
  96.3 1.4 second_gather.1
  97.7 10.7 %all_to_all.44.refs_0_ = f32[8,4,128]{2,1,0:T(4,128)S(1)} all-to-all(f32[8,4,128]{2,1,0:T(4,128)S(1)} %get-tuple-element.44), channel_id=1, replica_groups=mesh['sub'=64,'crs'=8] {'crs'}, dimensions={0} | all-to-all | bytes 32768 | tf_op jit(solution)/shard_map/all_to_all | solution.py:399
  108.4 0.5 second_direction.1
  108.9 17.8 %all_to_all.45.got_ref = bf16[64,4,128]{2,1,0:T(4,128)(2,1)S(1)} all-to-all(bf16[64,4,128]{2,1,0:T(4,128)(2,1)S(1)} %get-tuple-element.47), channel_id=1, replica_groups=mesh['sub'=64,'crs'=8] {'sub'}, dimensions={0} | all-to-all | bytes 131072 | tf_op jit(solution)/shard_map/all_to_all | solution.py:396
  126.7 0.0 copy-done.1
  126.7 1.0 second_operate.1
  127.7 9.0 %all_to_all.46.got_ref = f32[8,1,128]{2,1,0:T(1,128)S(1)} all-to-all(f32[8,1,128]{2,1,0:T(1,128)S(1)} %get-tuple-element.50), channel_id=1, replica_groups=mesh['sub'=64,'crs'=8] {'crs'}, dimensions={0} | all-to-all | bytes 8192 | tf_op jit(solution)/shard_map/all_to_all | solution.py:399
  136.7 17.4 %all_to_all.47.refs_0_ = f32[64,1,128]{2,1,0:T(1,128)S(1)} all-to-all(f32[64,1,128]{2,1,0:T(1,128)S(1)} %between.1), channel_id=1, replica_groups=mesh['sub'=64,'crs'=8] {'sub'}, dimensions={0} | all-to-all | bytes 65536 | tf_op jit(solution)/shard_map/all_to_all | solution.py:396
  154.0 1.0 last.1
  (1 shorter events, 0.0 us)
Async XLA Ops:
  1.3 0.7 copy-start
  77.3 49.4 %copy-start.1 = (s32[1,1,6]{2,1,0:T(1,128)S(1)}, s32[1,1,6]{2,1,0:T(1,128)}, u32[]{:S(2)}) copy-start(s32[1,1,6]{2,1,0:T(1,128)} %param.15) | copy-start | bytes 76

commit v4 on v3

--- a/solution.py
+++ b/solution.py
@@ -80,26 +80,27 @@
         out_ref[2 * i + 1, :, 0:LANES] = chosen[cols:].astype(jnp.bfloat16)
 
 
-def margin_from(got_ref, near_ref, live_ref, slots):
+def margin_from(got_ref, near_ref, slots):
+    near = near_ref[...]
     parts = []
     for j in range(slots):
-        part = got_ref[near_ref[j], :, 0:LANES]
-        parts.append(jnp.where(j < live_ref[0], part, jnp.zeros_like(part)))
+        source = near[0, j]
+        part = got_ref[jnp.maximum(source, 0), :, 0:LANES]
+        parts.append(jnp.where(source >= 0, part, jnp.zeros_like(part)))
     return jnp.concatenate(parts, axis=1)
 
 
 def first_send_kernel(
-    near, live, r_hbm, basis_hbm, picked_hbm, coarse_hbm, inverse_hbm, own_hbm, couple_hbm,
-    out_ref, r_ref, basis_ref, picked, coarse_ref, inverse_ref, own_ref, couple_ref, sems,
+    live, near_hbm, r_hbm, basis_hbm, picked_hbm, coarse_hbm, inverse_hbm,
+    out_ref, table_ref, r_ref, basis_ref, picked, coarse_ref, inverse_ref, near_ref, sems,
 ):
     pairs = [
         (r_hbm, r_ref),
         (basis_hbm, basis_ref),
         (picked_hbm, picked),
+        (near_hbm, near_ref),
         (coarse_hbm, coarse_ref),
         (inverse_hbm, inverse_ref),
-        (own_hbm, own_ref),
-        (couple_hbm, couple_ref),
     ]
     moves = [
         pltpu.make_async_copy(source, target, sems.at[i])
@@ -107,7 +108,7 @@
     ]
     for move in moves:
         move.start()
-    for move in moves[:3]:
+    for move in moves[:4]:
         move.wait()
     subs, cols, _ = out_ref.shape
     rows = r_ref.shape[2]
@@ -124,7 +125,10 @@
     sub = lax.broadcasted_iota(jnp.int32, (cols, LANES), 0)
     wide = LANES // cols
     slots = picked.shape[0]
-    for j in range(slots):
+    near = near_ref[...]
+    table = jnp.concatenate([near, jnp.zeros((1, LANES - slots), jnp.int32)], axis=1)
+    table_ref[...] = jnp.where(lanes_of((1, LANES)) < live[0, 0], table, -1)
+    for j in reversed(range(slots)):
         wanted = (picked[j] - rows // 2).astype(jnp.float32)
         wanted = jnp.broadcast_to(wanted, (cols, LANES))
         packed = jnp.zeros((cols, LANES), jnp.float32)
@@ -132,12 +136,8 @@
             moved = pltpu.roll(wanted, (kc - i * wide) % LANES, 1)
             packed = jnp.where(sub == i, moved, packed)
         packed = jnp.where((lane >= kc) & (lane < kc + wide), packed, tail)
-
-        @pl.when(j < live[0])
-        def _():
-            out_ref[near[j], :, rows : rows + LANES] = packed.astype(jnp.bfloat16)
-
-    for move in moves[3:]:
+        out_ref[near[0, j], :, rows : rows + LANES] = packed.astype(jnp.bfloat16)
+    for move in moves[4:]:
         move.wait()
 
 
@@ -182,19 +182,21 @@
 
 
 def first_gather_kernel(
-    near_ref, live_ref, r_ref, picked_ref, got_ref, inverse_ref, coarse_ref, fine_ref, asked_ref, out_ref
+    near_ref, r_ref, picked_ref, got_ref, inverse_ref, coarse_ref, fine_ref, asked_ref, out_ref
 ):
     subs, cols, _ = got_ref.shape
     rows = r_ref.shape[2]
     slots = picked_ref.shape[0]
     write_share(rows, False, got_ref, coarse_ref, out_ref)
+    near = near_ref[...]
     parts = [r_ref[:, 0, :].astype(jnp.bfloat16)]
     for j in range(slots):
-        near = got_ref[near_ref[j], :, 0:rows].astype(jnp.float32)
-        tiles = [twice(near[:, t * LANES : (t + 1) * LANES]) for t in range(rows // LANES)]
+        source = near[0, j]
+        other = got_ref[jnp.maximum(source, 0), :, 0:rows].astype(jnp.float32)
+        tiles = [twice(other[:, t * LANES : (t + 1) * LANES]) for t in range(rows // LANES)]
         index = jnp.broadcast_to(picked_ref[j], (2 * cols, LANES))
         part = pick_lanes(tiles, index)[:cols]
-        parts.append(jnp.where(j < live_ref[0], part, 0.0).astype(jnp.bfloat16))
+        parts.append(jnp.where(source >= 0, part, 0.0).astype(jnp.bfloat16))
     extended = jnp.concatenate(parts, axis=1)
     fine_ref[...] = lax.dot_general(
         extended, inverse_ref[...], LAST, preferred_element_type=jnp.float32
@@ -218,12 +220,12 @@
 
 
 def second_gather_kernel(
-    near_ref, live_ref, vector_ref, got_ref, inverse_ref, coarse_ref, fine_ref, out_ref
+    near_ref, vector_ref, got_ref, inverse_ref, coarse_ref, fine_ref, out_ref
 ):
     rows = vector_ref.shape[1]
     slots = (inverse_ref.shape[1] - rows) // LANES
     write_share(LANES, True, got_ref, coarse_ref, out_ref)
-    margin = margin_from(got_ref, near_ref, live_ref, slots)
+    margin = margin_from(got_ref, near_ref, slots)
     extended = jnp.concatenate([vector_ref[...].astype(jnp.bfloat16), margin], axis=1)
     fine_ref[...] = lax.dot_general(
         extended, inverse_ref[...], LAST, preferred_element_type=jnp.float32
@@ -243,8 +245,8 @@
     send_rows(p, asked_ref, out_ref)
 
 
-def operate(near_ref, live_ref, vector_ref, got_ref, own_ref, coupling_ref):
-    margin = margin_from(got_ref, near_ref, live_ref, coupling_ref.shape[1] // LANES)
+def operate(near_ref, vector_ref, got_ref, own_ref, coupling_ref):
+    margin = margin_from(got_ref, near_ref, coupling_ref.shape[1] // LANES)
     low = vector_ref[...].astype(jnp.bfloat16)
     return lax.dot_general(
         low, own_ref[...], LAST, preferred_element_type=jnp.float32
@@ -256,11 +258,11 @@
 
 
 def first_operate_kernel(
-    near_ref, live_ref, p_ref, got_ref, own_ref, coupling_ref, r_ref, basis_ref, asked_ref, q_ref, out_ref
+    near_ref, p_ref, got_ref, own_ref, coupling_ref, r_ref, basis_ref, asked_ref, q_ref, out_ref
 ):
     cols = r_ref.shape[0]
     kc = basis_ref.shape[0]
-    q = operate(near_ref, live_ref, p_ref, got_ref, own_ref, coupling_ref)
+    q = operate(near_ref, p_ref, got_ref, own_ref, coupling_ref)
     q_ref[...] = q
     r = r_ref[:, 0, :]
     residual = lax.dot_general(
@@ -304,9 +306,9 @@
 
 
 def second_operate_kernel(
-    near_ref, live_ref, z_ref, got_ref, own_ref, coupling_ref, v1_ref, v2_ref, w_ref, out_ref
-):
-    w = operate(near_ref, live_ref, z_ref, got_ref, own_ref, coupling_ref)
+    near_ref, z_ref, got_ref, own_ref, coupling_ref, v1_ref, v2_ref, w_ref, out_ref
+):
+    w = operate(near_ref, z_ref, got_ref, own_ref, coupling_ref)
     w_ref[...] = w
     v1 = v1_ref[...]
     v2 = v2_ref[...]
@@ -348,13 +350,12 @@
     answer_ref[:, 0, :] = weights[0] * z1_ref[...] + weights[1] * z2_ref[...]
 
 
-def call(kernel, outs, *args, scalars=0, name):
-    smem = pl.BlockSpec(memory_space=pltpu.SMEM)
+def call(kernel, outs, *args, name):
     vmem = pl.BlockSpec(memory_space=pltpu.VMEM)
     return pl.pallas_call(
         kernel,
         out_shape=outs,
-        in_specs=[smem] * scalars + [vmem] * (len(args) - scalars),
+        in_specs=[vmem] * len(args),
         out_specs=jax.tree.map(lambda _: vmem, outs),
         compiler_params=pltpu.CompilerParams(vmem_limit_bytes=VMEM_BYTES),
         name=name,
@@ -379,9 +380,9 @@
     inverse = local_inverse[0, 0]
     basis = coarse_basis[0, 0]
     coarse = coarse_inverse[0, :, 0, :]
-    near = neighbours[0, 0]
+    near = neighbours[0]
     picked = margin_rows.reshape(margin_rows.shape[2], 1, margin_rows.shape[3])
-    live = block_counts[0]
+    live = block_counts
     subs, owners = lax.axis_size("sub"), lax.axis_size("crs")
     all_rows = rows * subs * owners
     f32, bf16 = jnp.float32, jnp.bfloat16
@@ -398,27 +399,24 @@
     def over_crs(blocks):
         return lax.all_to_all(blocks, "crs", 0, 0)
 
-    near_live = (near, live)
-    held = [r, basis, picked, coarse, inverse, own, couple]
+    held = [r, basis, picked, coarse, inverse]
     vmem = pl.BlockSpec(memory_space=pltpu.VMEM)
-    sent, r, basis, picked, coarse, inverse, own, couple = pl.pallas_call(
+    sent, near, r, basis, picked, coarse, inverse = pl.pallas_call(
         first_send_kernel,
-        out_shape=[shape(subs, cols, rows + LANES, dtype=bf16)]
+        out_shape=[shape(subs, cols, rows + LANES, dtype=bf16), shape(1, LANES, dtype=jnp.int32)]
         + [shape(*x.shape, dtype=x.dtype) for x in held],
-        in_specs=[pl.BlockSpec(memory_space=pltpu.SMEM)] * 2
-        + [pl.BlockSpec(memory_space=pltpu.HBM)] * 7,
-        out_specs=[vmem] * 8,
-        scratch_shapes=[
-            pltpu.SemaphoreType.DMA((7,)),
-        ],
+        in_specs=[pl.BlockSpec(memory_space=pltpu.SMEM)]
+        + [pl.BlockSpec(memory_space=pl.ANY)] * 6,
+        out_specs=[vmem] * 7,
+        scratch_shapes=[pltpu.VMEM(near.shape, jnp.int32), pltpu.SemaphoreType.DMA((6,))],
         compiler_params=pltpu.CompilerParams(vmem_limit_bytes=VMEM_BYTES),
         name="first_send",
-    )(near, live, *[pltpu.with_memory_space_constraint(x, pltpu.HBM) for x in held])
+    )(live, *[pltpu.with_memory_space_constraint(x, pltpu.HBM) for x in (near, *held)])
     got = over_sub(sent)
     fine, asked, shares = call(
         first_gather_kernel,
         (vector, shape(subs // 2, 2 * cols, LANES, dtype=jnp.int32), shape(owners, cols, LANES)),
-        *near_live, r, picked, got, inverse, coarse, scalars=2, name="first_gather",
+        near, r, picked, got, inverse, coarse, name="first_gather",
     )
     shares = over_crs(shares)
     p1, sent = call(
@@ -428,12 +426,12 @@
     got = over_sub(sent)
     q1, sent = call(
         first_operate_kernel, (vector, shape(subs, cols, 2 * LANES, dtype=bf16)),
-        *near_live, p1, got, own, couple, r, basis, asked, scalars=2, name="first_operate",
+        near, p1, got, own, couple, r, basis, asked, name="first_operate",
     )
     got = over_sub(sent)
     fine, shares = call(
         second_gather_kernel, (vector, shape(owners, cols, LANES)),
-        *near_live, q1, got, inverse, coarse, scalars=2, name="second_gather",
+        near, q1, got, inverse, coarse, name="second_gather",
     )
     shares = over_crs(shares)
 
@@ -448,7 +446,7 @@
     got = over_sub(sent)
     w, sent = call(
         second_operate_kernel, (vector, shape(owners, 1, LANES)),
-        *near_live, z2, got, own, couple, v1, v2, scalars=2, name="second_operate",
+        near, z2, got, own, couple, v1, v2, name="second_operate",
     )
     got = over_crs(sent)
     sent = call(between_kernel, shape(subs, 1, LANES), got, name="between")

time: 155 us -> 152 us (0.981)
  Pallas kernels: 9.48 us -> 6.67 us
    pallas_call x8, Pallas kernels: 6.9 us -> 4.87 us  [call(): pl.pallas_call(kernel, out_shape=outs, in_specs=[vmem] * len(args), out_s...]
where the time goes in v4:
time: 152 us
  blocking collectives  144 us (95%)
  Pallas kernels  6.67 us (4%)
    all_to_all x5, blocking collectives, over_sub(): return lax.all_to_all(blocks, 'sub', 0, 0)  111 us
    all_to_all x3, blocking collectives, over_crs(): return lax.all_to_all(blocks, 'crs', 0, 0)  33 us
    pallas_call x8, Pallas kernels, call(): pl.pallas_call(kernel, out_shape=outs, in_specs=[vmem] * len(args), out_s...  4.87 us

profile of v4, /device:TPU:1, one launch (start us, length us, event | category | flops | bytes accessed | tf_op | source)
XLA Modules:
  0.0 151.8 jit_solution(8828463922146647821)
XLA Ops:
  1.3 1.8 %first_send.1 = (bf16[64,4,512]{2,1,0:T(4,128)(2,1)S(1)}, s32[1,128]{1,0:T(1,128)S(1)}, f32[4,1,384]{2,1,0:T(1,128)S(1)}, f32[40,384]{1,0:T(8,128)S(1)}, s32[6,1...) custom-call(s32[1,1]{1,0:T(1,128)S(6)} %copy.13.live, s32[1,6]{1,0:T(1,128)} %bitcast.23, ...), custom_call_target="tpu_custom_call" | custom-call | tf_op jit(solution)/shard_map/first_send/pallas_call | solution.py:404
  3.1 38.1 %all_to_all.40.got_ref = bf16[64,4,512]{2,1,0:T(4,128)(2,1)S(1)} all-to-all(bf16[64,4,512]{2,1,0:T(4,128)(2,1)S(1)} %get-tuple-element.31), channel_id=1, replica_groups=mesh['sub'=64,'crs'=8] {'sub'}, dimensions={0} | all-to-all | bytes 524288 | tf_op jit(solution)/shard_map/all_to_all | solution.py:397
  41.2 0.0 copy-start
  41.2 0.0 copy-start.1
  41.2 0.9 first_gather.1
  42.1 13.1 %all_to_all.41.shares_ref = f32[8,4,128]{2,1,0:T(4,128)S(1)} all-to-all(f32[8,4,128]{2,1,0:T(4,128)S(1)} %get-tuple-element.34), channel_id=1, replica_groups=mesh['sub'=64,'crs'=8] {'crs'}, dimensions={0} | all-to-all | bytes 32768 | tf_op jit(solution)/shard_map/all_to_all | solution.py:400
  55.2 0.4 first_direction.1
  55.6 18.5 %all_to_all.42.got_ref = bf16[64,4,128]{2,1,0:T(4,128)(2,1)S(1)} all-to-all(bf16[64,4,128]{2,1,0:T(4,128)(2,1)S(1)} %get-tuple-element.39), channel_id=1, replica_groups=mesh['sub'=64,'crs'=8] {'sub'}, dimensions={0} | all-to-all | bytes 131072 | tf_op jit(solution)/shard_map/all_to_all | solution.py:397
  74.1 0.0 copy-done
  74.1 0.0 copy-done.1
  74.1 0.7 first_operate.1
  74.9 18.9 %all_to_all.43.got_ref = bf16[64,4,256]{2,1,0:T(4,128)(2,1)S(1)} all-to-all(bf16[64,4,256]{2,1,0:T(4,128)(2,1)S(1)} %get-tuple-element.41), channel_id=1, replica_groups=mesh['sub'=64,'crs'=8] {'sub'}, dimensions={0} | all-to-all | bytes 262144 | tf_op jit(solution)/shard_map/all_to_all | solution.py:397
  93.8 0.9 second_gather.1
  94.7 10.7 %all_to_all.44.refs_0_ = f32[8,4,128]{2,1,0:T(4,128)S(1)} all-to-all(f32[8,4,128]{2,1,0:T(4,128)S(1)} %get-tuple-element.42), channel_id=1, replica_groups=mesh['sub'=64,'crs'=8] {'crs'}, dimensions={0} | all-to-all | bytes 32768 | tf_op jit(solution)/shard_map/all_to_all | solution.py:400
  105.4 0.5 second_direction.1
  105.9 17.8 %all_to_all.45.got_ref = bf16[64,4,128]{2,1,0:T(4,128)(2,1)S(1)} all-to-all(bf16[64,4,128]{2,1,0:T(4,128)(2,1)S(1)} %get-tuple-element.45), channel_id=1, replica_groups=mesh['sub'=64,'crs'=8] {'sub'}, dimensions={0} | all-to-all | bytes 131072 | tf_op jit(solution)/shard_map/all_to_all | solution.py:397
  123.7 0.5 second_operate.1
  124.2 9.2 %all_to_all.46.got_ref = f32[8,1,128]{2,1,0:T(1,128)S(1)} all-to-all(f32[8,1,128]{2,1,0:T(1,128)S(1)} %get-tuple-element.48), channel_id=1, replica_groups=mesh['sub'=64,'crs'=8] {'crs'}, dimensions={0} | all-to-all | bytes 8192 | tf_op jit(solution)/shard_map/all_to_all | solution.py:400
  133.4 17.4 %all_to_all.47.refs_0_ = f32[64,1,128]{2,1,0:T(1,128)S(1)} all-to-all(f32[64,1,128]{2,1,0:T(1,128)S(1)} %between.1), channel_id=1, replica_groups=mesh['sub'=64,'crs'=8] {'sub'}, dimensions={0} | all-to-all | bytes 65536 | tf_op jit(solution)/shard_map/all_to_all | solution.py:397
  150.8 1.0 last.1
  (1 shorter events, 0.0 us)
Async XLA Ops:
  41.2 32.9 %copy-start = (bf16[1,1,384,768]{3,2,1,0:T(8,128)(2,1)S(1)}, bf16[1,1,384,768]{3,2,1,0:T(8,128)(2,1)}, u32[]{:S(2)}) copy-start(bf16[1,1,384,768]{3,2,1,0:T(8,128)(2,1)} %param.11) | copy-start | bytes 1769476
  41.2 32.9 %copy-start.1 = (bf16[1,1,384,384]{3,2,1,0:T(8,128)(2,1)S(1)}, bf16[1,1,384,384]{3,2,1,0:T(8,128)(2,1)}, u32[]{:S(2)}) copy-start(bf16[1,1,384,384]{3,2,1,0:T(8,128)(2,1)} %param.10) | copy-start | bytes 884740

commit v5 on v4

--- a/solution.py
+++ b/solution.py
@@ -6,7 +6,7 @@
 from jax.sharding import PartitionSpec as P
 
 EPS = 1e-06
-HIGH = lax.Precision.HIGHEST
+HIGH = lax.Precision.HIGH
 LAST = (((1,), (1,)), ((), ()))
 FIRST = (((1,), (0,)), ((), ()))
 LANES = 128
@@ -91,16 +91,14 @@
 
 
 def first_send_kernel(
-    live, near_hbm, r_hbm, basis_hbm, picked_hbm, coarse_hbm, inverse_hbm,
-    out_ref, table_ref, r_ref, basis_ref, picked, coarse_ref, inverse_ref, near_ref, sems,
+    live, near_hbm, r_hbm, basis_hbm, picked_hbm,
+    out_ref, table_ref, r_ref, basis_ref, picked, near_ref, sems,
 ):
     pairs = [
         (r_hbm, r_ref),
         (basis_hbm, basis_ref),
         (picked_hbm, picked),
         (near_hbm, near_ref),
-        (coarse_hbm, coarse_ref),
-        (inverse_hbm, inverse_ref),
     ]
     moves = [
         pltpu.make_async_copy(source, target, sems.at[i])
@@ -182,7 +180,7 @@
 
 
 def first_gather_kernel(
-    near_ref, r_ref, picked_ref, got_ref, inverse_ref, coarse_ref, fine_ref, asked_ref, out_ref
+    near_ref, r_ref, picked_ref, got_ref, coarse_ref, extended_ref, asked_ref, out_ref
 ):
     subs, cols, _ = got_ref.shape
     rows = r_ref.shape[2]
@@ -197,10 +195,7 @@
         index = jnp.broadcast_to(picked_ref[j], (2 * cols, LANES))
         part = pick_lanes(tiles, index)[:cols]
         parts.append(jnp.where(source >= 0, part, 0.0).astype(jnp.bfloat16))
-    extended = jnp.concatenate(parts, axis=1)
-    fine_ref[...] = lax.dot_general(
-        extended, inverse_ref[...], LAST, preferred_element_type=jnp.float32
-    )
+    extended_ref[...] = jnp.concatenate(parts, axis=1)
     lane = lanes_of((cols, LANES))
     kc = coarse_ref.shape[0] // out_ref.shape[0]
     wide = LANES // cols
@@ -220,27 +215,27 @@
 
 
 def second_gather_kernel(
-    near_ref, vector_ref, got_ref, inverse_ref, coarse_ref, fine_ref, out_ref
+    near_ref, vector_ref, got_ref, coarse_ref, extended_ref, out_ref
 ):
     rows = vector_ref.shape[1]
-    slots = (inverse_ref.shape[1] - rows) // LANES
+    slots = (extended_ref.shape[1] - rows) // LANES
     write_share(LANES, True, got_ref, coarse_ref, out_ref)
     margin = margin_from(got_ref, near_ref, slots)
-    extended = jnp.concatenate([vector_ref[...].astype(jnp.bfloat16), margin], axis=1)
-    fine_ref[...] = lax.dot_general(
-        extended, inverse_ref[...], LAST, preferred_element_type=jnp.float32
-    )
-
-
-def prolong(summed, fine_ref, basis_ref):
+    extended_ref[...] = jnp.concatenate([vector_ref[...].astype(jnp.bfloat16), margin], axis=1)
+
+
+def prolong(summed, extended_ref, inverse_ref, basis_ref):
     kc = basis_ref.shape[0]
-    return fine_ref[...] + lax.dot_general(
+    fine = lax.dot_general(
+        extended_ref[...], inverse_ref[...], LAST, preferred_element_type=jnp.float32
+    )
+    return fine + lax.dot_general(
         summed[:, :kc], basis_ref[...], FIRST, precision=HIGH, preferred_element_type=jnp.float32
     )
 
 
-def first_direction_kernel(shares_ref, fine_ref, basis_ref, asked_ref, p_ref, out_ref):
-    p = prolong(jnp.sum(shares_ref[...], axis=0), fine_ref, basis_ref)
+def first_direction_kernel(shares_ref, extended_ref, inverse_ref, basis_ref, asked_ref, p_ref, out_ref):
+    p = prolong(jnp.sum(shares_ref[...], axis=0), extended_ref, inverse_ref, basis_ref)
     p_ref[...] = p
     send_rows(p, asked_ref, out_ref)
 
@@ -280,12 +275,12 @@
 
 
 def second_direction_kernel(
-    all_rows, shares_ref, fine_ref, basis_ref, asked_ref, r_ref, q_ref, p_ref,
+    all_rows, shares_ref, extended_ref, inverse_ref, basis_ref, asked_ref, r_ref, q_ref, p_ref,
     v1_ref, v2_ref, z1_ref, z2_ref, scalars_ref, out_ref,
 ):
     kc = basis_ref.shape[0]
     summed = jnp.sum(shares_ref[...], axis=0)
-    p2 = prolong(summed, fine_ref, basis_ref)
+    p2 = prolong(summed, extended_ref, inverse_ref, basis_ref)
     rr, qr, qq = [summed[:, kc + i : kc + i + 1] / all_rows for i in range(3)]
     start = jnp.sqrt(rr + EPS)
     h11 = qr / start / start
@@ -332,7 +327,8 @@
     cols = w_ref.shape[0]
     lane = lanes_of((cols, LANES))
     col = lax.broadcasted_iota(jnp.int32, (cols, LANES), 0)
-    inner = jnp.broadcast_to(jnp.sum(got_ref[...], axis=0) / all_rows, (cols, LANES))
+    inner = jnp.sum(got_ref[...], axis=0, keepdims=True) / all_rows
+    inner = jnp.broadcast_to(inner, (cols, LANES))
     h12, h22, ww, g11, g12, g22 = [
         row_sum(jnp.where(lane == i * cols + col, inner, 0.0)) for i in range(6)
     ]
@@ -399,29 +395,36 @@
     def over_crs(blocks):
         return lax.all_to_all(blocks, "crs", 0, 0)
 
-    held = [r, basis, picked, coarse, inverse]
+    held = [r, basis, picked]
     vmem = pl.BlockSpec(memory_space=pltpu.VMEM)
-    sent, near, r, basis, picked, coarse, inverse = pl.pallas_call(
+    sent, near, r, basis, picked = pl.pallas_call(
         first_send_kernel,
         out_shape=[shape(subs, cols, rows + LANES, dtype=bf16), shape(1, LANES, dtype=jnp.int32)]
         + [shape(*x.shape, dtype=x.dtype) for x in held],
         in_specs=[pl.BlockSpec(memory_space=pltpu.SMEM)]
-        + [pl.BlockSpec(memory_space=pl.ANY)] * 6,
-        out_specs=[vmem] * 7,
-        scratch_shapes=[pltpu.VMEM(near.shape, jnp.int32), pltpu.SemaphoreType.DMA((6,))],
+        + [pl.BlockSpec(memory_space=pl.ANY)] * 4,
+        out_specs=[vmem] * 5,
+        scratch_shapes=[pltpu.VMEM(near.shape, jnp.int32), pltpu.SemaphoreType.DMA((8,))],
         compiler_params=pltpu.CompilerParams(vmem_limit_bytes=VMEM_BYTES),
+        cost_estimate=pl.CostEstimate(
+            flops=1 << 34, bytes_accessed=1 << 30, transcendentals=0
+        ),
         name="first_send",
     )(live, *[pltpu.with_memory_space_constraint(x, pltpu.HBM) for x in (near, *held)])
     got = over_sub(sent)
-    fine, asked, shares = call(
+    extended, asked, shares = call(
         first_gather_kernel,
-        (vector, shape(subs // 2, 2 * cols, LANES, dtype=jnp.int32), shape(owners, cols, LANES)),
-        near, r, picked, got, inverse, coarse, name="first_gather",
+        (
+            shape(cols, inverse.shape[1], dtype=bf16),
+            shape(subs // 2, 2 * cols, LANES, dtype=jnp.int32),
+            shape(owners, cols, LANES),
+        ),
+        near, r, picked, got, coarse, name="first_gather",
     )
     shares = over_crs(shares)
     p1, sent = call(
         first_direction_kernel, (vector, shape(subs, cols, LANES, dtype=bf16)),
-        shares, fine, basis, asked, name="first_direction",
+        shares, extended, inverse, basis, asked, name="first_direction",
     )
     got = over_sub(sent)
     q1, sent = call(
@@ -429,9 +432,10 @@
         near, p1, got, own, couple, r, basis, asked, name="first_operate",
     )
     got = over_sub(sent)
-    fine, shares = call(
-        second_gather_kernel, (vector, shape(owners, cols, LANES)),
-        near, q1, got, inverse, coarse, name="second_gather",
+    extended, shares = call(
+        second_gather_kernel,
+        (shape(cols, inverse.shape[1], dtype=bf16), shape(owners, cols, LANES)),
+        near, q1, got, coarse, name="second_gather",
     )
     shares = over_crs(shares)
 
@@ -441,7 +445,7 @@
     v1, v2, z1, z2, scalars, sent = call(
         second_direction,
         (vector, vector, vector, vector, tile, shape(subs, cols, LANES, dtype=bf16)),
-        shares, fine, basis, asked, r, q1, p1, name="second_direction",
+        shares, extended, inverse, basis, asked, r, q1, p1, name="second_direction",
     )
     got = over_sub(sent)
     w, sent = call(
@@ -450,7 +454,7 @@
     )
     got = over_crs(sent)
     sent = call(between_kernel, shape(subs, 1, LANES), got, name="between")
-    got = over_sub(sent)
+    got = over_sub(sent).reshape(subs, LANES)
 
     def last(*refs):
         last_kernel(float(all_rows), *refs)

time: 152 us -> 151 us (level)
  no operation moved by 1% of the time
where the time goes in v5:
time: 151 us
  blocking collectives  144 us (95%)
  Pallas kernels  5.84 us (4%)
    all_to_all x5, blocking collectives, over_sub(): return lax.all_to_all(blocks, 'sub', 0, 0)  111 us
    all_to_all x3, blocking collectives, over_crs(): return lax.all_to_all(blocks, 'crs', 0, 0)  33 us
    pallas_call x8, Pallas kernels, call(): pl.pallas_call(kernel, out_shape=outs, in_specs=[vmem] * len(args), out_s...  4.62 us

profile of v5, /device:TPU:1, one launch (start us, length us, event | category | flops | bytes accessed | tf_op | source)
XLA Modules:
  0.0 151.1 jit_solution(15195784482532677394)
XLA Ops:
  1.3 0.0 copy-start
  1.3 1.2 first_send.1
  2.5 0.0 copy-start.1
  2.5 38.2 %all_to_all.40.got_ref = bf16[64,4,512]{2,1,0:T(4,128)(2,1)S(1)} all-to-all(bf16[64,4,512]{2,1,0:T(4,128)(2,1)S(1)} %get-tuple-element.29), channel_id=1, replica_groups=mesh['sub'=64,'crs'=8] {'sub'}, dimensions={0} | all-to-all | bytes 524288 | tf_op jit(solution)/shard_map/all_to_all | solution.py:393
  40.8 0.0 copy-start.2
  40.8 0.0 copy-start.3
  40.8 0.0 copy-done
  40.8 0.6 first_gather.1
  41.4 13.1 %all_to_all.41.shares_ref = f32[8,4,128]{2,1,0:T(4,128)S(1)} all-to-all(f32[8,4,128]{2,1,0:T(4,128)S(1)} %get-tuple-element.30), channel_id=1, replica_groups=mesh['sub'=64,'crs'=8] {'crs'}, dimensions={0} | all-to-all | bytes 32768 | tf_op jit(solution)/shard_map/all_to_all | solution.py:396
  54.5 0.0 copy-done.1
  54.5 0.6 first_direction.1
  55.2 18.5 %all_to_all.42.got_ref = bf16[64,4,128]{2,1,0:T(4,128)(2,1)S(1)} all-to-all(bf16[64,4,128]{2,1,0:T(4,128)(2,1)S(1)} %get-tuple-element.35), channel_id=1, replica_groups=mesh['sub'=64,'crs'=8] {'sub'}, dimensions={0} | all-to-all | bytes 131072 | tf_op jit(solution)/shard_map/all_to_all | solution.py:393
  73.7 0.0 copy-done.2
  73.7 0.0 copy-done.3
  73.7 0.7 first_operate.1
  74.3 18.9 %all_to_all.43.got_ref = bf16[64,4,256]{2,1,0:T(4,128)(2,1)S(1)} all-to-all(bf16[64,4,256]{2,1,0:T(4,128)(2,1)S(1)} %get-tuple-element.37), channel_id=1, replica_groups=mesh['sub'=64,'crs'=8] {'sub'}, dimensions={0} | all-to-all | bytes 262144 | tf_op jit(solution)/shard_map/all_to_all | solution.py:393
  93.3 0.6 second_gather.1
  93.9 10.7 %all_to_all.44.refs_0_ = f32[8,4,128]{2,1,0:T(4,128)S(1)} all-to-all(f32[8,4,128]{2,1,0:T(4,128)S(1)} %get-tuple-element.38), channel_id=1, replica_groups=mesh['sub'=64,'crs'=8] {'crs'}, dimensions={0} | all-to-all | bytes 32768 | tf_op jit(solution)/shard_map/all_to_all | solution.py:396
  104.6 0.6 second_direction.1
  105.2 17.8 %all_to_all.45.got_ref = bf16[64,4,128]{2,1,0:T(4,128)(2,1)S(1)} all-to-all(bf16[64,4,128]{2,1,0:T(4,128)(2,1)S(1)} %get-tuple-element.41), channel_id=1, replica_groups=mesh['sub'=64,'crs'=8] {'sub'}, dimensions={0} | all-to-all | bytes 131072 | tf_op jit(solution)/shard_map/all_to_all | solution.py:393
  123.1 0.5 second_operate.1
  123.6 9.2 %all_to_all.46.got_ref = f32[8,1,128]{2,1,0:T(1,128)S(1)} all-to-all(f32[8,1,128]{2,1,0:T(1,128)S(1)} %get-tuple-element.44), channel_id=1, replica_groups=mesh['sub'=64,'crs'=8] {'crs'}, dimensions={0} | all-to-all | bytes 8192 | tf_op jit(solution)/shard_map/all_to_all | solution.py:396
  132.7 17.4 %all_to_all.47 = f32[64,1,128]{2,1,0:T(1,128)S(1)} all-to-all(f32[64,1,128]{2,1,0:T(1,128)S(1)} %between.1), channel_id=1, replica_groups=mesh['sub'=64,'crs'=8] {'sub'}, dimensions={0} | all-to-all | bytes 65536 | tf_op jit(solution)/shard_map/all_to_all | solution.py:393
  150.1 0.9 last.1
  (1 shorter events, 0.0 us)
Async XLA Ops:
  1.3 39.5 %copy-start = (bf16[1,320,1,2560]{3,1,2,0:T(8,128)(2,1)S(1)}, bf16[1,320,1,2560]{3,1,2,0:T(8,128)(2,1)}, u32[]{:S(2)}) copy-start(bf16[1,320,1,2560]{3,1,2,0:T(8,128)(2,1)} %param.14) | copy-start | bytes 4915204
  2.5 52.0 %copy-start.1 = (bf16[1,1,384,1152]{3,2,1,0:T(8,128)(2,1)S(1)}, bf16[1,1,384,1152]{3,2,1,0:T(8,128)(2,1)}, u32[]{:S(2)}) copy-start(bf16[1,1,384,1152]{3,2,1,0:T(8,128)(2,1)} %param.12) | copy-start | bytes 2654212
  40.8 32.9 %copy-start.2 = (bf16[1,1,384,768]{3,2,1,0:T(8,128)(2,1)S(1)}, bf16[1,1,384,768]{3,2,1,0:T(8,128)(2,1)}, u32[]{:S(2)}) copy-start(bf16[1,1,384,768]{3,2,1,0:T(8,128)(2,1)} %param.11) | copy-start | bytes 1769476
  40.8 32.9 %copy-start.3 = (bf16[1,1,384,384]{3,2,1,0:T(8,128)(2,1)S(1)}, bf16[1,1,384,384]{3,2,1,0:T(8,128)(2,1)}, u32[]{:S(2)}) copy-start(bf16[1,1,384,384]{3,2,1,0:T(8,128)(2,1)} %param.10) | copy-start | bytes 884740

commit v6 on v5

--- a/solution.py
+++ b/solution.py
@@ -11,6 +11,18 @@
 FIRST = (((1,), (0,)), ((), ()))
 LANES = 128
 VMEM_BYTES = 16 << 20
+PLANES = 16
+NEAR = 4
+STRIDE = 7
+BACK = pow(STRIDE, -1, PLANES)
+
+
+def order_of(subs):
+    return [STRIDE * (i // NEAR) % PLANES * NEAR + i % NEAR for i in range(subs)]
+
+
+def place_of(sub):
+    return (((sub >> 2) * BACK) & (PLANES - 1)) * NEAR + (sub & (NEAR - 1))
 
 
 def least_squares(start_norm, columns):
@@ -123,7 +135,7 @@
     sub = lax.broadcasted_iota(jnp.int32, (cols, LANES), 0)
     wide = LANES // cols
     slots = picked.shape[0]
-    near = near_ref[...]
+    near = place_of(near_ref[...])
     table = jnp.concatenate([near, jnp.zeros((1, LANES - slots), jnp.int32)], axis=1)
     table_ref[...] = jnp.where(lanes_of((1, LANES)) < live[0, 0], table, -1)
     for j in reversed(range(slots)):
@@ -146,8 +158,8 @@
     lane = lanes_of((cols, LANES))
     tiles = [jnp.zeros((cols, LANES), jnp.float32) for _ in range(subs * kc // LANES)]
     terms = jnp.zeros((cols, LANES), jnp.float32)
-    for s in range(subs):
-        got = got_ref[s, :, at : at + LANES].astype(jnp.float32)
+    for block, s in enumerate(order_of(subs)):
+        got = got_ref[block, :, at : at + LANES].astype(jnp.float32)
         if with_terms:
             terms = terms + got
         t, off = divmod(s * kc, LANES)
@@ -390,7 +402,7 @@
     tile = shape(cols, LANES)
 
     def over_sub(blocks):
-        return lax.all_to_all(blocks, "sub", 0, 0)
+        return lax.all_to_all(blocks, "sub", 0, 0, axis_index_groups=[order_of(subs)])
 
     def over_crs(blocks):
         return lax.all_to_all(blocks, "crs", 0, 0)

time: 151 us -> 150 us (level)
  no operation moved by 1% of the time
where the time goes in v6:
time: 150 us
  blocking collectives  143 us (95%)
  Pallas kernels  5.83 us (4%)
    all_to_all x5, blocking collectives, over_sub(): lax.all_to_all(blocks, 'sub', 0, 0, axis_index_groups=[order_of(subs)])  111 us
    all_to_all x3, blocking collectives, over_crs(): return lax.all_to_all(blocks, 'crs', 0, 0)  32 us
    pallas_call x8, Pallas kernels, call(): pl.pallas_call(kernel, out_shape=outs, in_specs=[vmem] * len(args), out_s...  4.62 us

profile of v6, /device:TPU:1, one launch (start us, length us, event | category | flops | bytes accessed | tf_op | source)
XLA Modules:
  0.0 149.9 jit_solution(639762512575391257)
XLA Ops:
  1.3 0.0 copy-start
  1.3 1.2 first_send.1
  2.5 0.0 copy-start.1
  2.5 38.7 %all_to_all.40.got_ref = bf16[64,4,512]{2,1,0:T(4,128)(2,1)S(1)} all-to-all(bf16[64,4,512]{2,1,0:T(4,128)(2,1)S(1)} %get-tuple-element.29), channel_id=1, replica_groups={{0,8,16,24,224,232,240,248,448,456,464,472,160,168,176,184,384,392,400,..., dimensions={0} | all-to-all | bytes 524288 | tf_op jit(solution)/shard_map/all_to_all | solution.py:405
  41.2 0.0 copy-start.2
  41.2 0.0 copy-start.3
  41.2 0.0 copy-done
  41.2 0.6 first_gather.1
  41.8 12.4 %all_to_all.41.shares_ref = f32[8,4,128]{2,1,0:T(4,128)S(1)} all-to-all(f32[8,4,128]{2,1,0:T(4,128)S(1)} %get-tuple-element.30), channel_id=1, replica_groups=mesh['sub'=64,'crs'=8] {'crs'}, dimensions={0} | all-to-all | bytes 32768 | tf_op jit(solution)/shard_map/all_to_all | solution.py:408
  54.2 0.0 copy-done.1
  54.2 0.6 first_direction.1
  54.8 18.5 %all_to_all.42.got_ref = bf16[64,4,128]{2,1,0:T(4,128)(2,1)S(1)} all-to-all(bf16[64,4,128]{2,1,0:T(4,128)(2,1)S(1)} %get-tuple-element.35), channel_id=1, replica_groups={{0,8,16,24,224,232,240,248,448,456,464,472,160,168,176,184,384,392,400,..., dimensions={0} | all-to-all | bytes 131072 | tf_op jit(solution)/shard_map/all_to_all | solution.py:405
  73.3 0.0 copy-done.2
  73.3 0.0 copy-done.3
  73.3 0.7 first_operate.1
  73.9 18.6 %all_to_all.43.got_ref = bf16[64,4,256]{2,1,0:T(4,128)(2,1)S(1)} all-to-all(bf16[64,4,256]{2,1,0:T(4,128)(2,1)S(1)} %get-tuple-element.37), channel_id=1, replica_groups={{0,8,16,24,224,232,240,248,448,456,464,472,160,168,176,184,384,392,400,..., dimensions={0} | all-to-all | bytes 262144 | tf_op jit(solution)/shard_map/all_to_all | solution.py:405
  92.6 0.6 second_gather.1
  93.2 11.0 %all_to_all.44.refs_0_ = f32[8,4,128]{2,1,0:T(4,128)S(1)} all-to-all(f32[8,4,128]{2,1,0:T(4,128)S(1)} %get-tuple-element.38), channel_id=1, replica_groups=mesh['sub'=64,'crs'=8] {'crs'}, dimensions={0} | all-to-all | bytes 32768 | tf_op jit(solution)/shard_map/all_to_all | solution.py:408
  104.3 0.6 second_direction.1
  104.9 17.8 %all_to_all.45.got_ref = bf16[64,4,128]{2,1,0:T(4,128)(2,1)S(1)} all-to-all(bf16[64,4,128]{2,1,0:T(4,128)(2,1)S(1)} %get-tuple-element.41), channel_id=1, replica_groups={{0,8,16,24,224,232,240,248,448,456,464,472,160,168,176,184,384,392,400,..., dimensions={0} | all-to-all | bytes 131072 | tf_op jit(solution)/shard_map/all_to_all | solution.py:405
  122.7 0.5 second_operate.1
  123.2 8.6 %all_to_all.46.got_ref = f32[8,1,128]{2,1,0:T(1,128)S(1)} all-to-all(f32[8,1,128]{2,1,0:T(1,128)S(1)} %get-tuple-element.44), channel_id=1, replica_groups=mesh['sub'=64,'crs'=8] {'crs'}, dimensions={0} | all-to-all | bytes 8192 | tf_op jit(solution)/shard_map/all_to_all | solution.py:408
  131.8 17.2 %all_to_all.47 = f32[64,1,128]{2,1,0:T(1,128)S(1)} all-to-all(f32[64,1,128]{2,1,0:T(1,128)S(1)} %between.1), channel_id=1, replica_groups={{0,8,16,24,224,232,240,248,448,456,464,472,160,168,176,184,384,392,400,..., dimensions={0} | all-to-all | bytes 65536 | tf_op jit(solution)/shard_map/all_to_all | solution.py:405
  149.0 0.9 last.1
  (1 shorter events, 0.0 us)
Async XLA Ops:
  1.3 39.9 %copy-start = (bf16[1,320,1,2560]{3,1,2,0:T(8,128)(2,1)S(1)}, bf16[1,320,1,2560]{3,1,2,0:T(8,128)(2,1)}, u32[]{:S(2)}) copy-start(bf16[1,320,1,2560]{3,1,2,0:T(8,128)(2,1)} %param.14) | copy-start | bytes 4915204
  2.5 51.7 %copy-start.1 = (bf16[1,1,384,1152]{3,2,1,0:T(8,128)(2,1)S(1)}, bf16[1,1,384,1152]{3,2,1,0:T(8,128)(2,1)}, u32[]{:S(2)}) copy-start(bf16[1,1,384,1152]{3,2,1,0:T(8,128)(2,1)} %param.12) | copy-start | bytes 2654212
  41.2 32.1 %copy-start.2 = (bf16[1,1,384,768]{3,2,1,0:T(8,128)(2,1)S(1)}, bf16[1,1,384,768]{3,2,1,0:T(8,128)(2,1)}, u32[]{:S(2)}) copy-start(bf16[1,1,384,768]{3,2,1,0:T(8,128)(2,1)} %param.11) | copy-start | bytes 1769476
  41.2 32.1 %copy-start.3 = (bf16[1,1,384,384]{3,2,1,0:T(8,128)(2,1)S(1)}, bf16[1,1,384,384]{3,2,1,0:T(8,128)(2,1)}, u32[]{:S(2)}) copy-start(bf16[1,1,384,384]{3,2,1,0:T(8,128)(2,1)} %param.10) | copy-start | bytes 884740

commit v7 on v6

--- a/solution.py
+++ b/solution.py
@@ -61,6 +61,16 @@
     return hi, mid, rest - mid
 
 
+def halves(x):
+    hi = x.astype(jnp.bfloat16)
+    return jnp.concatenate([hi, (x - hi.astype(jnp.float32)).astype(jnp.bfloat16)], axis=0)
+
+
+def joined(x):
+    rows = x.shape[0] // 2
+    return x[:rows] + x[rows:]
+
+
 def place(column, lane, at):
     return jnp.where(lane == at, column, 0.0)
 
@@ -199,7 +209,7 @@
     slots = picked_ref.shape[0]
     write_share(rows, False, got_ref, coarse_ref, out_ref)
     near = near_ref[...]
-    parts = [r_ref[:, 0, :].astype(jnp.bfloat16)]
+    parts = []
     for j in range(slots):
         source = near[0, j]
         other = got_ref[jnp.maximum(source, 0), :, 0:rows].astype(jnp.float32)
@@ -207,7 +217,8 @@
         index = jnp.broadcast_to(picked_ref[j], (2 * cols, LANES))
         part = pick_lanes(tiles, index)[:cols]
         parts.append(jnp.where(source >= 0, part, 0.0).astype(jnp.bfloat16))
-    extended_ref[...] = jnp.concatenate(parts, axis=1)
+    margin = jnp.concatenate(parts, axis=1)
+    extended_ref[...] = extend(r_ref[:, 0, :], margin)
     lane = lanes_of((cols, LANES))
     kc = coarse_ref.shape[0] // out_ref.shape[0]
     wide = LANES // cols
@@ -233,7 +244,7 @@
     slots = (extended_ref.shape[1] - rows) // LANES
     write_share(LANES, True, got_ref, coarse_ref, out_ref)
     margin = margin_from(got_ref, near_ref, slots)
-    extended_ref[...] = jnp.concatenate([vector_ref[...].astype(jnp.bfloat16), margin], axis=1)
+    extended_ref[...] = extend(vector_ref[...], margin)
 
 
 def prolong(summed, extended_ref, inverse_ref, basis_ref):
@@ -241,7 +252,7 @@
     fine = lax.dot_general(
         extended_ref[...], inverse_ref[...], LAST, preferred_element_type=jnp.float32
     )
-    return fine + lax.dot_general(
+    return joined(fine) + lax.dot_general(
         summed[:, :kc], basis_ref[...], FIRST, precision=HIGH, preferred_element_type=jnp.float32
     )
 
@@ -254,10 +265,14 @@
 
 def operate(near_ref, vector_ref, got_ref, own_ref, coupling_ref):
     margin = margin_from(got_ref, near_ref, coupling_ref.shape[1] // LANES)
-    low = vector_ref[...].astype(jnp.bfloat16)
-    return lax.dot_general(
-        low, own_ref[...], LAST, preferred_element_type=jnp.float32
-    ) + lax.dot_general(margin, coupling_ref[...], LAST, preferred_element_type=jnp.float32)
+    own = lax.dot_general(
+        halves(vector_ref[...]), own_ref[...], LAST, preferred_element_type=jnp.float32
+    )
+    return joined(own) + lax.dot_general(margin, coupling_ref[...], LAST, preferred_element_type=jnp.float32)
+
+
+def extend(vector, margin):
+    return jnp.concatenate([halves(vector), jnp.concatenate([margin, jnp.zeros_like(margin)])], axis=1)
 
 
 def row_sum(x):
@@ -427,7 +442,7 @@
     extended, asked, shares = call(
         first_gather_kernel,
         (
-            shape(cols, inverse.shape[1], dtype=bf16),
+            shape(2 * cols, inverse.shape[1], dtype=bf16),
             shape(subs // 2, 2 * cols, LANES, dtype=jnp.int32),
             shape(owners, cols, LANES),
         ),
@@ -446,7 +461,7 @@
     got = over_sub(sent)
     extended, shares = call(
         second_gather_kernel,
-        (shape(cols, inverse.shape[1], dtype=bf16), shape(owners, cols, LANES)),
+        (shape(2 * cols, inverse.shape[1], dtype=bf16), shape(owners, cols, LANES)),
         near, q1, got, coarse, name="second_gather",
     )
     shares = over_crs(shares)

time: 150 us -> 150 us (level)
  no operation moved by 1% of the time
where the time goes in v7:
time: 150 us
  blocking collectives  143 us (95%)
  Pallas kernels  5.77 us (4%)
    all_to_all x5, blocking collectives, over_sub(): lax.all_to_all(blocks, 'sub', 0, 0, axis_index_groups=[order_of(subs)])  111 us
    all_to_all x3, blocking collectives, over_crs(): return lax.all_to_all(blocks, 'crs', 0, 0)  32 us
    pallas_call x8, Pallas kernels, call(): pl.pallas_call(kernel, out_shape=outs, in_specs=[vmem] * len(args), out_s...  4.56 us

profile of v7, /device:TPU:1, one launch (start us, length us, event | category | flops | bytes accessed | tf_op | source)
XLA Modules:
  0.0 149.9 jit_solution(6057784407723116198)
XLA Ops:
  1.3 0.0 copy-start
  1.3 1.2 first_send.1
  2.5 0.0 copy-start.1
  2.5 38.7 %all_to_all.40.got_ref = bf16[64,4,512]{2,1,0:T(4,128)(2,1)S(1)} all-to-all(bf16[64,4,512]{2,1,0:T(4,128)(2,1)S(1)} %get-tuple-element.29), channel_id=1, replica_groups={{0,8,16,24,224,232,240,248,448,456,464,472,160,168,176,184,384,392,400,..., dimensions={0} | all-to-all | bytes 524288 | tf_op jit(solution)/shard_map/all_to_all | solution.py:420
  41.2 0.0 copy-start.2
  41.2 0.0 copy-start.3
  41.2 0.0 copy-done
  41.2 0.6 first_gather.1
  41.8 12.4 %all_to_all.41.shares_ref = f32[8,4,128]{2,1,0:T(4,128)S(1)} all-to-all(f32[8,4,128]{2,1,0:T(4,128)S(1)} %get-tuple-element.30), channel_id=1, replica_groups=mesh['sub'=64,'crs'=8] {'crs'}, dimensions={0} | all-to-all | bytes 32768 | tf_op jit(solution)/shard_map/all_to_all | solution.py:423
  54.2 0.0 copy-done.1
  54.2 0.6 first_direction.1
  54.8 18.4 %all_to_all.42.got_ref = bf16[64,4,128]{2,1,0:T(4,128)(2,1)S(1)} all-to-all(bf16[64,4,128]{2,1,0:T(4,128)(2,1)S(1)} %get-tuple-element.35), channel_id=1, replica_groups={{0,8,16,24,224,232,240,248,448,456,464,472,160,168,176,184,384,392,400,..., dimensions={0} | all-to-all | bytes 131072 | tf_op jit(solution)/shard_map/all_to_all | solution.py:420
  73.3 0.0 copy-done.2
  73.3 0.0 copy-done.3
  73.3 0.6 first_operate.1
  73.9 18.6 %all_to_all.43.got_ref = bf16[64,4,256]{2,1,0:T(4,128)(2,1)S(1)} all-to-all(bf16[64,4,256]{2,1,0:T(4,128)(2,1)S(1)} %get-tuple-element.37), channel_id=1, replica_groups={{0,8,16,24,224,232,240,248,448,456,464,472,160,168,176,184,384,392,400,..., dimensions={0} | all-to-all | bytes 262144 | tf_op jit(solution)/shard_map/all_to_all | solution.py:420
  92.6 0.6 second_gather.1
  93.2 11.1 %all_to_all.44.refs_0_ = f32[8,4,128]{2,1,0:T(4,128)S(1)} all-to-all(f32[8,4,128]{2,1,0:T(4,128)S(1)} %get-tuple-element.38), channel_id=1, replica_groups=mesh['sub'=64,'crs'=8] {'crs'}, dimensions={0} | all-to-all | bytes 32768 | tf_op jit(solution)/shard_map/all_to_all | solution.py:423
  104.3 0.6 second_direction.1
  104.9 17.8 %all_to_all.45.got_ref = bf16[64,4,128]{2,1,0:T(4,128)(2,1)S(1)} all-to-all(bf16[64,4,128]{2,1,0:T(4,128)(2,1)S(1)} %get-tuple-element.41), channel_id=1, replica_groups={{0,8,16,24,224,232,240,248,448,456,464,472,160,168,176,184,384,392,400,..., dimensions={0} | all-to-all | bytes 131072 | tf_op jit(solution)/shard_map/all_to_all | solution.py:420
  122.7 0.5 second_operate.1
  123.1 8.6 %all_to_all.46.got_ref = f32[8,1,128]{2,1,0:T(1,128)S(1)} all-to-all(f32[8,1,128]{2,1,0:T(1,128)S(1)} %get-tuple-element.44), channel_id=1, replica_groups=mesh['sub'=64,'crs'=8] {'crs'}, dimensions={0} | all-to-all | bytes 8192 | tf_op jit(solution)/shard_map/all_to_all | solution.py:423
  131.8 17.2 %all_to_all.47 = f32[64,1,128]{2,1,0:T(1,128)S(1)} all-to-all(f32[64,1,128]{2,1,0:T(1,128)S(1)} %between.1), channel_id=1, replica_groups={{0,8,16,24,224,232,240,248,448,456,464,472,160,168,176,184,384,392,400,..., dimensions={0} | all-to-all | bytes 65536 | tf_op jit(solution)/shard_map/all_to_all | solution.py:420
  148.9 0.9 last.1
  (1 shorter events, 0.0 us)
Async XLA Ops:
  1.3 39.9 %copy-start = (bf16[1,320,1,2560]{3,1,2,0:T(8,128)(2,1)S(1)}, bf16[1,320,1,2560]{3,1,2,0:T(8,128)(2,1)}, u32[]{:S(2)}) copy-start(bf16[1,320,1,2560]{3,1,2,0:T(8,128)(2,1)} %param.14) | copy-start | bytes 4915204
  2.5 51.7 %copy-start.1 = (bf16[1,1,384,1152]{3,2,1,0:T(8,128)(2,1)S(1)}, bf16[1,1,384,1152]{3,2,1,0:T(8,128)(2,1)}, u32[]{:S(2)}) copy-start(bf16[1,1,384,1152]{3,2,1,0:T(8,128)(2,1)} %param.12) | copy-start | bytes 2654212
  41.2 32.1 %copy-start.2 = (bf16[1,1,384,768]{3,2,1,0:T(8,128)(2,1)S(1)}, bf16[1,1,384,768]{3,2,1,0:T(8,128)(2,1)}, u32[]{:S(2)}) copy-start(bf16[1,1,384,768]{3,2,1,0:T(8,128)(2,1)} %param.11) | copy-start | bytes 1769476
  41.2 32.1 %copy-start.3 = (bf16[1,1,384,384]{3,2,1,0:T(8,128)(2,1)S(1)}, bf16[1,1,384,384]{3,2,1,0:T(8,128)(2,1)}, u32[]{:S(2)}) copy-start(bf16[1,1,384,384]{3,2,1,0:T(8,128)(2,1)} %param.10) | copy-start | bytes 884740

commit v8 on v7

--- a/solution.py
+++ b/solution.py
@@ -96,20 +96,28 @@
 def send_rows(vector, asked_ref, out_ref):
     tiles = [twice(vector[:, t * LANES : (t + 1) * LANES]) for t in range(vector.shape[1] // LANES)]
     cols = vector.shape[0]
+    height = out_ref.shape[1]
     for i in range(asked_ref.shape[0]):
         chosen = pick_lanes(tiles, asked_ref[i])
-        out_ref[2 * i, :, 0:LANES] = chosen[:cols].astype(jnp.bfloat16)
-        out_ref[2 * i + 1, :, 0:LANES] = chosen[cols:].astype(jnp.bfloat16)
-
-
-def margin_from(got_ref, near_ref, slots):
+        for at in range(0, 2 * cols, height):
+            part, t = divmod(at, cols)
+            lanes = pl.ds(t // height * LANES, LANES)
+            out_ref[2 * i + part, :, lanes] = chosen[at : at + height].astype(jnp.bfloat16)
+
+
+def margin_from(got_ref, near_ref, slots, cols):
     near = near_ref[...]
     parts = []
     for j in range(slots):
         source = near[0, j]
-        part = got_ref[jnp.maximum(source, 0), :, 0:LANES]
-        parts.append(jnp.where(source >= 0, part, jnp.zeros_like(part)))
-    return jnp.concatenate(parts, axis=1)
+        part = got_ref[jnp.maximum(source, 0)]
+        parts.append(jnp.where(source >= 0, part, jnp.zeros_like(part)).astype(jnp.float32))
+    width = cols // got_ref.shape[1]
+    columns = [
+        jnp.concatenate([part[:, t * LANES : (t + 1) * LANES] for part in parts], axis=1)
+        for t in range(width)
+    ]
+    return jnp.concatenate(columns, axis=0).astype(jnp.bfloat16)
 
 
 def first_send_kernel(
@@ -162,24 +170,33 @@
 
 
 def write_share(at, with_terms, got_ref, coarse_ref, out_ref):
-    subs, cols, _ = got_ref.shape
-    owners = out_ref.shape[0]
+    subs, height, _ = got_ref.shape
+    owners, cols, _ = out_ref.shape
     kc = coarse_ref.shape[0] // owners
-    lane = lanes_of((cols, LANES))
-    tiles = [jnp.zeros((cols, LANES), jnp.float32) for _ in range(subs * kc // LANES)]
-    terms = jnp.zeros((cols, LANES), jnp.float32)
+    lane = lanes_of((height, LANES))
+    width = cols // height
+    zero = jnp.zeros((height, LANES), jnp.float32)
+    tiles = [[zero] * (subs * kc // LANES) for _ in range(width)]
+    terms = zero
     for block, s in enumerate(order_of(subs)):
         got = got_ref[block, :, at : at + LANES].astype(jnp.float32)
         if with_terms:
             terms = terms + got
         t, off = divmod(s * kc, LANES)
-        moved = pltpu.roll(got, off, 1) if off else got
-        if off + kc <= LANES:
-            tiles[t] = jnp.where((lane >= off) & (lane < off + kc), moved, tiles[t])
-        else:
-            tiles[t] = jnp.where(lane >= off, moved, tiles[t])
-            tiles[t + 1] = jnp.where(lane < off + kc - LANES, moved, tiles[t + 1])
-    residuals = jnp.concatenate(tiles, axis=1).astype(jnp.bfloat16)
+        for part in range(width):
+            mine = tiles[part]
+            turn = (off - part * (LANES // width)) % LANES
+            moved = pltpu.roll(got, turn, 1) if turn else got
+            if off + kc <= LANES:
+                mine[t] = jnp.where((lane >= off) & (lane < off + kc), moved, mine[t])
+            else:
+                mine[t] = jnp.where(lane >= off, moved, mine[t])
+                mine[t + 1] = jnp.where(lane < off + kc - LANES, moved, mine[t + 1])
+    residuals = [jnp.concatenate(mine, axis=1) for mine in tiles]
+    residuals = jnp.concatenate(residuals, axis=0).astype(jnp.bfloat16)
+    if width > 1:
+        terms = jnp.concatenate([terms, pltpu.roll(terms, LANES // width, 1)], axis=0)
+    lane = lanes_of((cols, LANES))
     share = lax.dot_general(
         residuals, coarse_ref[...], LAST, preferred_element_type=jnp.float32
     )
@@ -242,8 +259,8 @@
 ):
     rows = vector_ref.shape[1]
     slots = (extended_ref.shape[1] - rows) // LANES
-    write_share(LANES, True, got_ref, coarse_ref, out_ref)
-    margin = margin_from(got_ref, near_ref, slots)
+    write_share(2 * LANES, True, got_ref, coarse_ref, out_ref)
+    margin = margin_from(got_ref, near_ref, slots, vector_ref.shape[0])
     extended_ref[...] = extend(vector_ref[...], margin)
 
 
@@ -264,7 +281,8 @@
 
 
 def operate(near_ref, vector_ref, got_ref, own_ref, coupling_ref):
-    margin = margin_from(got_ref, near_ref, coupling_ref.shape[1] // LANES)
+    slots = coupling_ref.shape[1] // LANES
+    margin = margin_from(got_ref, near_ref, slots, vector_ref.shape[0])
     own = lax.dot_general(
         halves(vector_ref[...]), own_ref[...], LAST, preferred_element_type=jnp.float32
     )
@@ -296,8 +314,10 @@
         for k, term in enumerate(split3(inner)):
             tail = jnp.where(lane == kc + 3 * k + i, term, tail)
     send_rows(q, asked_ref, out_ref)
-    out_ref[:, :, LANES : 2 * LANES] = jnp.broadcast_to(
-        tail.astype(jnp.bfloat16)[None], (out_ref.shape[0], cols, LANES)
+    half = cols // 2
+    tail = tail[:half] + pltpu.roll(tail[half:], LANES // 2, 1)
+    out_ref[:, :, 2 * LANES : 3 * LANES] = jnp.broadcast_to(
+        tail.astype(jnp.bfloat16)[None], (out_ref.shape[0], half, LANES)
     )
 
 
@@ -455,7 +475,7 @@
     )
     got = over_sub(sent)
     q1, sent = call(
-        first_operate_kernel, (vector, shape(subs, cols, 2 * LANES, dtype=bf16)),
+        first_operate_kernel, (vector, shape(subs, cols // 2, 3 * LANES, dtype=bf16)),
         near, p1, got, own, couple, r, basis, asked, name="first_operate",
     )
     got = over_sub(sent)

time: 150 us -> 150 us (level)
  no operation moved by 1% of the time
where the time goes in v8:
time: 150 us; the launch traced here: 149 us
  blocking collectives  142 us (95%)
  Pallas kernels  5.79 us (4%)
    all_to_all x5, blocking collectives, over_sub(): lax.all_to_all(blocks, 'sub', 0, 0, axis_index_groups=[order_of(subs)])  110 us
    all_to_all x3, blocking collectives, over_crs(): return lax.all_to_all(blocks, 'crs', 0, 0)  31.9 us
    pallas_call x8, Pallas kernels, call(): pl.pallas_call(kernel, out_shape=outs, in_specs=[vmem] * len(args), out_s...  4.58 us

profile of v8, /device:TPU:1, one launch (start us, length us, event | category | flops | bytes accessed | tf_op | source)
XLA Modules:
  0.0 149.4 jit_solution(4826422782246535141)
XLA Ops:
  1.3 0.0 copy-start
  1.3 1.2 first_send.1
  2.5 0.0 copy-start.1
  2.5 38.7 %all_to_all.40.got_ref = bf16[64,4,512]{2,1,0:T(4,128)(2,1)S(1)} all-to-all(bf16[64,4,512]{2,1,0:T(4,128)(2,1)S(1)} %get-tuple-element.29), channel_id=1, replica_groups={{0,8,16,24,224,232,240,248,448,456,464,472,160,168,176,184,384,392,400,..., dimensions={0} | all-to-all | bytes 524288 | tf_op jit(solution)/shard_map/all_to_all | solution.py:440
  41.2 0.0 copy-start.2
  41.2 0.0 copy-start.3
  41.2 0.0 copy-done
  41.2 0.6 first_gather.1
  41.8 12.4 %all_to_all.41.shares_ref = f32[8,4,128]{2,1,0:T(4,128)S(1)} all-to-all(f32[8,4,128]{2,1,0:T(4,128)S(1)} %get-tuple-element.30), channel_id=1, replica_groups=mesh['sub'=64,'crs'=8] {'crs'}, dimensions={0} | all-to-all | bytes 32768 | tf_op jit(solution)/shard_map/all_to_all | solution.py:443
  54.2 0.0 copy-done.1
  54.2 0.6 first_direction.1
  54.8 18.4 %all_to_all.42.got_ref = bf16[64,4,128]{2,1,0:T(4,128)(2,1)S(1)} all-to-all(bf16[64,4,128]{2,1,0:T(4,128)(2,1)S(1)} %get-tuple-element.35), channel_id=1, replica_groups={{0,8,16,24,224,232,240,248,448,456,464,472,160,168,176,184,384,392,400,..., dimensions={0} | all-to-all | bytes 131072 | tf_op jit(solution)/shard_map/all_to_all | solution.py:440
  73.3 0.0 copy-done.2
  73.3 0.0 copy-done.3
  73.3 0.6 first_operate.1
  73.9 18.2 %all_to_all.43.got_ref = bf16[64,2,384]{2,1,0:T(2,128)(2,1)S(1)} all-to-all(bf16[64,2,384]{2,1,0:T(2,128)(2,1)S(1)} %get-tuple-element.37), channel_id=1, replica_groups={{0,8,16,24,224,232,240,248,448,456,464,472,160,168,176,184,384,392,400,..., dimensions={0} | all-to-all | bytes 196608 | tf_op jit(solution)/shard_map/all_to_all | solution.py:440
  92.2 0.6 second_gather.1
  92.8 10.8 %all_to_all.44.refs_0_ = f32[8,4,128]{2,1,0:T(4,128)S(1)} all-to-all(f32[8,4,128]{2,1,0:T(4,128)S(1)} %get-tuple-element.38), channel_id=1, replica_groups=mesh['sub'=64,'crs'=8] {'crs'}, dimensions={0} | all-to-all | bytes 32768 | tf_op jit(solution)/shard_map/all_to_all | solution.py:443
  103.6 0.6 second_direction.1
  104.2 17.8 %all_to_all.45.got_ref = bf16[64,4,128]{2,1,0:T(4,128)(2,1)S(1)} all-to-all(bf16[64,4,128]{2,1,0:T(4,128)(2,1)S(1)} %get-tuple-element.41), channel_id=1, replica_groups={{0,8,16,24,224,232,240,248,448,456,464,472,160,168,176,184,384,392,400,..., dimensions={0} | all-to-all | bytes 131072 | tf_op jit(solution)/shard_map/all_to_all | solution.py:440
  122.0 0.5 second_operate.1
  122.5 8.7 %all_to_all.46.got_ref = f32[8,1,128]{2,1,0:T(1,128)S(1)} all-to-all(f32[8,1,128]{2,1,0:T(1,128)S(1)} %get-tuple-element.44), channel_id=1, replica_groups=mesh['sub'=64,'crs'=8] {'crs'}, dimensions={0} | all-to-all | bytes 8192 | tf_op jit(solution)/shard_map/all_to_all | solution.py:443
  131.3 17.2 %all_to_all.47 = f32[64,1,128]{2,1,0:T(1,128)S(1)} all-to-all(f32[64,1,128]{2,1,0:T(1,128)S(1)} %between.1), channel_id=1, replica_groups={{0,8,16,24,224,232,240,248,448,456,464,472,160,168,176,184,384,392,400,..., dimensions={0} | all-to-all | bytes 65536 | tf_op jit(solution)/shard_map/all_to_all | solution.py:440
  148.5 0.9 last.1
  (1 shorter events, 0.0 us)
Async XLA Ops:
  1.3 39.9 %copy-start = (bf16[1,320,1,2560]{3,1,2,0:T(8,128)(2,1)S(1)}, bf16[1,320,1,2560]{3,1,2,0:T(8,128)(2,1)}, u32[]{:S(2)}) copy-start(bf16[1,320,1,2560]{3,1,2,0:T(8,128)(2,1)} %param.14) | copy-start | bytes 4915204
  2.5 51.7 %copy-start.1 = (bf16[1,1,384,1152]{3,2,1,0:T(8,128)(2,1)S(1)}, bf16[1,1,384,1152]{3,2,1,0:T(8,128)(2,1)}, u32[]{:S(2)}) copy-start(bf16[1,1,384,1152]{3,2,1,0:T(8,128)(2,1)} %param.12) | copy-start | bytes 2654212
  41.2 32.1 %copy-start.2 = (bf16[1,1,384,768]{3,2,1,0:T(8,128)(2,1)S(1)}, bf16[1,1,384,768]{3,2,1,0:T(8,128)(2,1)}, u32[]{:S(2)}) copy-start(bf16[1,1,384,768]{3,2,1,0:T(8,128)(2,1)} %param.11) | copy-start | bytes 1769476
  41.2 32.1 %copy-start.3 = (bf16[1,1,384,384]{3,2,1,0:T(8,128)(2,1)S(1)}, bf16[1,1,384,384]{3,2,1,0:T(8,128)(2,1)}, u32[]{:S(2)}) copy-start(bf16[1,1,384,384]{3,2,1,0:T(8,128)(2,1)} %param.10) | copy-start | bytes 884740

commit v9 on v8

--- a/solution.py
+++ b/solution.py
@@ -13,16 +13,14 @@
 VMEM_BYTES = 16 << 20
 PLANES = 16
 NEAR = 4
-STRIDE = 7
-BACK = pow(STRIDE, -1, PLANES)
-
-
 def order_of(subs):
-    return [STRIDE * (i // NEAR) % PLANES * NEAR + i % NEAR for i in range(subs)]
+    planes = [i // (2 * NEAR) + i // NEAR % 2 * (PLANES // 2) for i in range(subs)]
+    return [plane * NEAR + i % NEAR for i, plane in enumerate(planes)]
 
 
 def place_of(sub):
-    return (((sub >> 2) * BACK) & (PLANES - 1)) * NEAR + (sub & (NEAR - 1))
+    plane = sub >> 2
+    return (((plane & 7) << 1) | (plane >> 3)) * NEAR + (sub & (NEAR - 1))
 
 
 def least_squares(start_norm, columns):

time: 150 us -> 149 us (level)
  no operation moved by 1% of the time
where the time goes in v9:
time: 149 us
  blocking collectives  142 us (95%)
  Pallas kernels  5.78 us (4%)
    all_to_all x5, blocking collectives, over_sub(): lax.all_to_all(blocks, 'sub', 0, 0, axis_index_groups=[order_of(subs)])  110 us
    all_to_all x3, blocking collectives, over_crs(): return lax.all_to_all(blocks, 'crs', 0, 0)  32 us
    pallas_call x8, Pallas kernels, call(): pl.pallas_call(kernel, out_shape=outs, in_specs=[vmem] * len(args), out_s...  4.57 us

profile of v9, /device:TPU:1, one launch (start us, length us, event | category | flops | bytes accessed | tf_op | source)
XLA Modules:
  0.0 148.7 jit_solution(17856664237890061511)
XLA Ops:
  1.3 0.0 copy-start
  1.3 1.2 first_send.1
  2.5 0.0 copy-start.1
  2.5 38.7 %all_to_all.40.got_ref = bf16[64,4,512]{2,1,0:T(4,128)(2,1)S(1)} all-to-all(bf16[64,4,512]{2,1,0:T(4,128)(2,1)S(1)} %get-tuple-element.29), channel_id=1, replica_groups={{0,8,16,24,256,264,272,280,32,40,48,56,288,296,304,312,64,72,80,88,320,..., dimensions={0} | all-to-all | bytes 524288 | tf_op jit(solution)/shard_map/all_to_all | solution.py:438
  41.2 0.0 copy-start.2
  41.2 0.0 copy-start.3
  41.2 0.0 copy-done
  41.2 0.6 first_gather.1
  41.9 12.1 %all_to_all.41.shares_ref = f32[8,4,128]{2,1,0:T(4,128)S(1)} all-to-all(f32[8,4,128]{2,1,0:T(4,128)S(1)} %get-tuple-element.30), channel_id=1, replica_groups=mesh['sub'=64,'crs'=8] {'crs'}, dimensions={0} | all-to-all | bytes 32768 | tf_op jit(solution)/shard_map/all_to_all | solution.py:441
  54.0 0.0 copy-done.1
  54.0 0.6 first_direction.1
  54.6 18.4 %all_to_all.42.got_ref = bf16[64,4,128]{2,1,0:T(4,128)(2,1)S(1)} all-to-all(bf16[64,4,128]{2,1,0:T(4,128)(2,1)S(1)} %get-tuple-element.35), channel_id=1, replica_groups={{0,8,16,24,256,264,272,280,32,40,48,56,288,296,304,312,64,72,80,88,320,..., dimensions={0} | all-to-all | bytes 131072 | tf_op jit(solution)/shard_map/all_to_all | solution.py:438
  73.0 0.0 copy-done.2
  73.0 0.0 copy-done.3
  73.1 0.6 first_operate.1
  73.7 18.3 %all_to_all.43.got_ref = bf16[64,2,384]{2,1,0:T(2,128)(2,1)S(1)} all-to-all(bf16[64,2,384]{2,1,0:T(2,128)(2,1)S(1)} %get-tuple-element.37), channel_id=1, replica_groups={{0,8,16,24,256,264,272,280,32,40,48,56,288,296,304,312,64,72,80,88,320,..., dimensions={0} | all-to-all | bytes 196608 | tf_op jit(solution)/shard_map/all_to_all | solution.py:438
  91.9 0.6 second_gather.1
  92.6 10.4 %all_to_all.44.refs_0_ = f32[8,4,128]{2,1,0:T(4,128)S(1)} all-to-all(f32[8,4,128]{2,1,0:T(4,128)S(1)} %get-tuple-element.38), channel_id=1, replica_groups=mesh['sub'=64,'crs'=8] {'crs'}, dimensions={0} | all-to-all | bytes 32768 | tf_op jit(solution)/shard_map/all_to_all | solution.py:441
  103.0 0.6 second_direction.1
  103.7 17.4 %all_to_all.45.got_ref = bf16[64,4,128]{2,1,0:T(4,128)(2,1)S(1)} all-to-all(bf16[64,4,128]{2,1,0:T(4,128)(2,1)S(1)} %get-tuple-element.41), channel_id=1, replica_groups={{0,8,16,24,256,264,272,280,32,40,48,56,288,296,304,312,64,72,80,88,320,..., dimensions={0} | all-to-all | bytes 131072 | tf_op jit(solution)/shard_map/all_to_all | solution.py:438
  121.1 0.5 second_operate.1
  121.6 9.5 %all_to_all.46.got_ref = f32[8,1,128]{2,1,0:T(1,128)S(1)} all-to-all(f32[8,1,128]{2,1,0:T(1,128)S(1)} %get-tuple-element.44), channel_id=1, replica_groups=mesh['sub'=64,'crs'=8] {'crs'}, dimensions={0} | all-to-all | bytes 8192 | tf_op jit(solution)/shard_map/all_to_all | solution.py:441
  131.1 16.7 %all_to_all.47 = f32[64,1,128]{2,1,0:T(1,128)S(1)} all-to-all(f32[64,1,128]{2,1,0:T(1,128)S(1)} %between.1), channel_id=1, replica_groups={{0,8,16,24,256,264,272,280,32,40,48,56,288,296,304,312,64,72,80,88,320,..., dimensions={0} | all-to-all | bytes 65536 | tf_op jit(solution)/shard_map/all_to_all | solution.py:438
  147.8 0.9 last.1
  (1 shorter events, 0.0 us)
Async XLA Ops:
  1.3 40.0 %copy-start = (bf16[1,320,1,2560]{3,1,2,0:T(8,128)(2,1)S(1)}, bf16[1,320,1,2560]{3,1,2,0:T(8,128)(2,1)}, u32[]{:S(2)}) copy-start(bf16[1,320,1,2560]{3,1,2,0:T(8,128)(2,1)} %param.14) | copy-start | bytes 4915204
  2.5 51.5 %copy-start.1 = (bf16[1,1,384,1152]{3,2,1,0:T(8,128)(2,1)S(1)}, bf16[1,1,384,1152]{3,2,1,0:T(8,128)(2,1)}, u32[]{:S(2)}) copy-start(bf16[1,1,384,1152]{3,2,1,0:T(8,128)(2,1)} %param.12) | copy-start | bytes 2654212
  41.2 31.8 %copy-start.2 = (bf16[1,1,384,768]{3,2,1,0:T(8,128)(2,1)S(1)}, bf16[1,1,384,768]{3,2,1,0:T(8,128)(2,1)}, u32[]{:S(2)}) copy-start(bf16[1,1,384,768]{3,2,1,0:T(8,128)(2,1)} %param.11) | copy-start | bytes 1769476
  41.2 31.8 %copy-start.3 = (bf16[1,1,384,384]{3,2,1,0:T(8,128)(2,1)S(1)}, bf16[1,1,384,384]{3,2,1,0:T(8,128)(2,1)}, u32[]{:S(2)}) copy-start(bf16[1,1,384,384]{3,2,1,0:T(8,128)(2,1)} %param.10) | copy-start | bytes 884740

commit v10 on v9

--- a/solution.py
+++ b/solution.py
@@ -14,13 +14,13 @@
 PLANES = 16
 NEAR = 4
 def order_of(subs):
-    planes = [i // (2 * NEAR) + i // NEAR % 2 * (PLANES // 2) for i in range(subs)]
-    return [plane * NEAR + i % NEAR for i, plane in enumerate(planes)]
+    planes = [i // (2 * NEAR) + i % 2 * (PLANES // 2) for i in range(subs)]
+    return [plane * NEAR + i // 2 % NEAR for i, plane in enumerate(planes)]
 
 
 def place_of(sub):
     plane = sub >> 2
-    return (((plane & 7) << 1) | (plane >> 3)) * NEAR + (sub & (NEAR - 1))
+    return (plane & 7) * (2 * NEAR) + (sub & (NEAR - 1)) * 2 + (plane >> 3)
 
 
 def least_squares(start_norm, columns):

time: 149 us -> 149 us (level)
  no operation moved by 1% of the time
where the time goes in v10:
time: 149 us
  blocking collectives  141 us (95%)
  Pallas kernels  5.79 us (4%)
    all_to_all x5, blocking collectives, over_sub(): lax.all_to_all(blocks, 'sub', 0, 0, axis_index_groups=[order_of(subs)])  109 us
    all_to_all x3, blocking collectives, over_crs(): return lax.all_to_all(blocks, 'crs', 0, 0)  32.2 us
    pallas_call x8, Pallas kernels, call(): pl.pallas_call(kernel, out_shape=outs, in_specs=[vmem] * len(args), out_s...  4.57 us

profile of v10, /device:TPU:1, one launch (start us, length us, event | category | flops | bytes accessed | tf_op | source)
XLA Modules:
  0.0 148.6 jit_solution(5253942391268244717)
XLA Ops:
  1.3 0.0 copy-start
  1.3 1.2 first_send.1
  2.5 0.0 copy-start.1
  2.5 39.3 %all_to_all.40.got_ref = bf16[64,4,512]{2,1,0:T(4,128)(2,1)S(1)} all-to-all(bf16[64,4,512]{2,1,0:T(4,128)(2,1)S(1)} %get-tuple-element.29), channel_id=1, replica_groups={{0,256,8,264,16,272,24,280,32,288,40,296,48,304,56,312,64,320,72,328,80..., dimensions={0} | all-to-all | bytes 524288 | tf_op jit(solution)/shard_map/all_to_all | solution.py:438
  41.8 0.0 copy-start.2
  41.8 0.0 copy-start.3
  41.8 0.0 copy-done
  41.8 0.6 first_gather.1
  42.4 12.2 %all_to_all.41.shares_ref = f32[8,4,128]{2,1,0:T(4,128)S(1)} all-to-all(f32[8,4,128]{2,1,0:T(4,128)S(1)} %get-tuple-element.30), channel_id=1, replica_groups=mesh['sub'=64,'crs'=8] {'crs'}, dimensions={0} | all-to-all | bytes 32768 | tf_op jit(solution)/shard_map/all_to_all | solution.py:441
  54.7 0.0 copy-done.1
  54.7 0.6 first_direction.1
  55.3 17.6 %all_to_all.42.got_ref = bf16[64,4,128]{2,1,0:T(4,128)(2,1)S(1)} all-to-all(bf16[64,4,128]{2,1,0:T(4,128)(2,1)S(1)} %get-tuple-element.35), channel_id=1, replica_groups={{0,256,8,264,16,272,24,280,32,288,40,296,48,304,56,312,64,320,72,328,80..., dimensions={0} | all-to-all | bytes 131072 | tf_op jit(solution)/shard_map/all_to_all | solution.py:438
  72.9 0.0 copy-done.2
  72.9 0.0 copy-done.3
  72.9 0.6 first_operate.1
  73.5 18.5 %all_to_all.43.got_ref = bf16[64,2,384]{2,1,0:T(2,128)(2,1)S(1)} all-to-all(bf16[64,2,384]{2,1,0:T(2,128)(2,1)S(1)} %get-tuple-element.37), channel_id=1, replica_groups={{0,256,8,264,16,272,24,280,32,288,40,296,48,304,56,312,64,320,72,328,80..., dimensions={0} | all-to-all | bytes 196608 | tf_op jit(solution)/shard_map/all_to_all | solution.py:438
  92.0 0.6 second_gather.1
  92.7 10.3 %all_to_all.44.refs_0_ = f32[8,4,128]{2,1,0:T(4,128)S(1)} all-to-all(f32[8,4,128]{2,1,0:T(4,128)S(1)} %get-tuple-element.38), channel_id=1, replica_groups=mesh['sub'=64,'crs'=8] {'crs'}, dimensions={0} | all-to-all | bytes 32768 | tf_op jit(solution)/shard_map/all_to_all | solution.py:441
  103.0 0.6 second_direction.1
  103.6 17.2 %all_to_all.45.got_ref = bf16[64,4,128]{2,1,0:T(4,128)(2,1)S(1)} all-to-all(bf16[64,4,128]{2,1,0:T(4,128)(2,1)S(1)} %get-tuple-element.41), channel_id=1, replica_groups={{0,256,8,264,16,272,24,280,32,288,40,296,48,304,56,312,64,320,72,328,80..., dimensions={0} | all-to-all | bytes 131072 | tf_op jit(solution)/shard_map/all_to_all | solution.py:438
  120.8 0.5 second_operate.1
  121.3 9.6 %all_to_all.46.got_ref = f32[8,1,128]{2,1,0:T(1,128)S(1)} all-to-all(f32[8,1,128]{2,1,0:T(1,128)S(1)} %get-tuple-element.44), channel_id=1, replica_groups=mesh['sub'=64,'crs'=8] {'crs'}, dimensions={0} | all-to-all | bytes 8192 | tf_op jit(solution)/shard_map/all_to_all | solution.py:441
  130.9 16.7 %all_to_all.47 = f32[64,1,128]{2,1,0:T(1,128)S(1)} all-to-all(f32[64,1,128]{2,1,0:T(1,128)S(1)} %between.1), channel_id=1, replica_groups={{0,256,8,264,16,272,24,280,32,288,40,296,48,304,56,312,64,320,72,328,80..., dimensions={0} | all-to-all | bytes 65536 | tf_op jit(solution)/shard_map/all_to_all | solution.py:438
  147.6 0.9 last.1
  (1 shorter events, 0.0 us)
Async XLA Ops:
  1.3 40.5 %copy-start = (bf16[1,320,1,2560]{3,1,2,0:T(8,128)(2,1)S(1)}, bf16[1,320,1,2560]{3,1,2,0:T(8,128)(2,1)}, u32[]{:S(2)}) copy-start(bf16[1,320,1,2560]{3,1,2,0:T(8,128)(2,1)} %param.14) | copy-start | bytes 4915204
  2.5 52.1 %copy-start.1 = (bf16[1,1,384,1152]{3,2,1,0:T(8,128)(2,1)S(1)}, bf16[1,1,384,1152]{3,2,1,0:T(8,128)(2,1)}, u32[]{:S(2)}) copy-start(bf16[1,1,384,1152]{3,2,1,0:T(8,128)(2,1)} %param.12) | copy-start | bytes 2654212
  41.8 31.1 %copy-start.2 = (bf16[1,1,384,768]{3,2,1,0:T(8,128)(2,1)S(1)}, bf16[1,1,384,768]{3,2,1,0:T(8,128)(2,1)}, u32[]{:S(2)}) copy-start(bf16[1,1,384,768]{3,2,1,0:T(8,128)(2,1)} %param.11) | copy-start | bytes 1769476
  41.8 31.1 %copy-start.3 = (bf16[1,1,384,384]{3,2,1,0:T(8,128)(2,1)S(1)}, bf16[1,1,384,384]{3,2,1,0:T(8,128)(2,1)}, u32[]{:S(2)}) copy-start(bf16[1,1,384,384]{3,2,1,0:T(8,128)(2,1)} %param.10) | copy-start | bytes 884740

commit v11 on v10

--- a/solution.py
+++ b/solution.py
@@ -13,14 +13,18 @@
 VMEM_BYTES = 16 << 20
 PLANES = 16
 NEAR = 4
+def turned(plane):
+    return ((plane & 1) << 2) | (plane & 2) | ((plane >> 2) & 1)
+
+
 def order_of(subs):
-    planes = [i // (2 * NEAR) + i % 2 * (PLANES // 2) for i in range(subs)]
+    planes = [turned(i // (2 * NEAR)) + i % 2 * (PLANES // 2) for i in range(subs)]
     return [plane * NEAR + i // 2 % NEAR for i, plane in enumerate(planes)]
 
 
 def place_of(sub):
     plane = sub >> 2
-    return (plane & 7) * (2 * NEAR) + (sub & (NEAR - 1)) * 2 + (plane >> 3)
+    return turned(plane & 7) * (2 * NEAR) + (sub & (NEAR - 1)) * 2 + (plane >> 3)
 
 
 def least_squares(start_norm, columns):

time: 149 us -> 149 us (level)
  no operation moved by 1% of the time
where the time goes in v11:
time: 149 us
  blocking collectives  141 us (95%)
  Pallas kernels  5.79 us (4%)
    all_to_all x5, blocking collectives, over_sub(): lax.all_to_all(blocks, 'sub', 0, 0, axis_index_groups=[order_of(subs)])  110 us
    all_to_all x3, blocking collectives, over_crs(): return lax.all_to_all(blocks, 'crs', 0, 0)  31.7 us
    pallas_call x8, Pallas kernels, call(): pl.pallas_call(kernel, out_shape=outs, in_specs=[vmem] * len(args), out_s...  4.58 us

profile of v11, /device:TPU:1, one launch (start us, length us, event | category | flops | bytes accessed | tf_op | source)
XLA Modules:
  0.0 148.6 jit_solution(1030266773392447835)
XLA Ops:
  1.3 0.0 copy-start
  1.3 1.2 first_send.1
  2.5 0.0 copy-start.1
  2.5 39.8 %all_to_all.40.got_ref = bf16[64,4,512]{2,1,0:T(4,128)(2,1)S(1)} all-to-all(bf16[64,4,512]{2,1,0:T(4,128)(2,1)S(1)} %get-tuple-element.29), channel_id=1, replica_groups={{0,256,8,264,16,272,24,280,128,384,136,392,144,400,152,408,64,320,72,32..., dimensions={0} | all-to-all | bytes 524288 | tf_op jit(solution)/shard_map/all_to_all | solution.py:442
  42.3 0.0 copy-start.2
  42.3 0.0 copy-start.3
  42.3 0.0 copy-done
  42.3 0.6 first_gather.1
  43.0 12.0 %all_to_all.41.shares_ref = f32[8,4,128]{2,1,0:T(4,128)S(1)} all-to-all(f32[8,4,128]{2,1,0:T(4,128)S(1)} %get-tuple-element.30), channel_id=1, replica_groups=mesh['sub'=64,'crs'=8] {'crs'}, dimensions={0} | all-to-all | bytes 32768 | tf_op jit(solution)/shard_map/all_to_all | solution.py:445
  55.0 0.0 copy-done.1
  55.0 0.6 first_direction.1
  55.6 17.8 %all_to_all.42.got_ref = bf16[64,4,128]{2,1,0:T(4,128)(2,1)S(1)} all-to-all(bf16[64,4,128]{2,1,0:T(4,128)(2,1)S(1)} %get-tuple-element.35), channel_id=1, replica_groups={{0,256,8,264,16,272,24,280,128,384,136,392,144,400,152,408,64,320,72,32..., dimensions={0} | all-to-all | bytes 131072 | tf_op jit(solution)/shard_map/all_to_all | solution.py:442
  73.4 0.0 copy-done.2
  73.4 0.0 copy-done.3
  73.4 0.6 first_operate.1
  74.0 18.2 %all_to_all.43.got_ref = bf16[64,2,384]{2,1,0:T(2,128)(2,1)S(1)} all-to-all(bf16[64,2,384]{2,1,0:T(2,128)(2,1)S(1)} %get-tuple-element.37), channel_id=1, replica_groups={{0,256,8,264,16,272,24,280,128,384,136,392,144,400,152,408,64,320,72,32..., dimensions={0} | all-to-all | bytes 196608 | tf_op jit(solution)/shard_map/all_to_all | solution.py:442
  92.2 0.6 second_gather.1
  92.9 10.5 %all_to_all.44.refs_0_ = f32[8,4,128]{2,1,0:T(4,128)S(1)} all-to-all(f32[8,4,128]{2,1,0:T(4,128)S(1)} %get-tuple-element.38), channel_id=1, replica_groups=mesh['sub'=64,'crs'=8] {'crs'}, dimensions={0} | all-to-all | bytes 32768 | tf_op jit(solution)/shard_map/all_to_all | solution.py:445
  103.4 0.6 second_direction.1
  104.0 17.2 %all_to_all.45.got_ref = bf16[64,4,128]{2,1,0:T(4,128)(2,1)S(1)} all-to-all(bf16[64,4,128]{2,1,0:T(4,128)(2,1)S(1)} %get-tuple-element.41), channel_id=1, replica_groups={{0,256,8,264,16,272,24,280,128,384,136,392,144,400,152,408,64,320,72,32..., dimensions={0} | all-to-all | bytes 131072 | tf_op jit(solution)/shard_map/all_to_all | solution.py:442
  121.2 0.5 second_operate.1
  121.7 9.2 %all_to_all.46.got_ref = f32[8,1,128]{2,1,0:T(1,128)S(1)} all-to-all(f32[8,1,128]{2,1,0:T(1,128)S(1)} %get-tuple-element.44), channel_id=1, replica_groups=mesh['sub'=64,'crs'=8] {'crs'}, dimensions={0} | all-to-all | bytes 8192 | tf_op jit(solution)/shard_map/all_to_all | solution.py:445
  130.9 16.7 %all_to_all.47 = f32[64,1,128]{2,1,0:T(1,128)S(1)} all-to-all(f32[64,1,128]{2,1,0:T(1,128)S(1)} %between.1), channel_id=1, replica_groups={{0,256,8,264,16,272,24,280,128,384,136,392,144,400,152,408,64,320,72,32..., dimensions={0} | all-to-all | bytes 65536 | tf_op jit(solution)/shard_map/all_to_all | solution.py:442
  147.6 0.9 last.1
  (1 shorter events, 0.0 us)
Async XLA Ops:
  1.3 41.1 %copy-start = (bf16[1,320,1,2560]{3,1,2,0:T(8,128)(2,1)S(1)}, bf16[1,320,1,2560]{3,1,2,0:T(8,128)(2,1)}, u32[]{:S(2)}) copy-start(bf16[1,320,1,2560]{3,1,2,0:T(8,128)(2,1)} %param.14) | copy-start | bytes 4915204
  2.5 52.5 %copy-start.1 = (bf16[1,1,384,1152]{3,2,1,0:T(8,128)(2,1)S(1)}, bf16[1,1,384,1152]{3,2,1,0:T(8,128)(2,1)}, u32[]{:S(2)}) copy-start(bf16[1,1,384,1152]{3,2,1,0:T(8,128)(2,1)} %param.12) | copy-start | bytes 2654212
  42.3 31.1 %copy-start.2 = (bf16[1,1,384,768]{3,2,1,0:T(8,128)(2,1)S(1)}, bf16[1,1,384,768]{3,2,1,0:T(8,128)(2,1)}, u32[]{:S(2)}) copy-start(bf16[1,1,384,768]{3,2,1,0:T(8,128)(2,1)} %param.11) | copy-start | bytes 1769476
  42.3 31.1 %copy-start.3 = (bf16[1,1,384,384]{3,2,1,0:T(8,128)(2,1)S(1)}, bf16[1,1,384,384]{3,2,1,0:T(8,128)(2,1)}, u32[]{:S(2)}) copy-start(bf16[1,1,384,384]{3,2,1,0:T(8,128)(2,1)} %param.10) | copy-start | bytes 884740
